TPU v7x, 256 devices: a whole 4x4x8 slice. The times are simulated.
256 devices in a mesh: row: 8 (over x, core), col: 32 (over z, y).
Axes of the slice: x: 4, y: 4, z: 8, core: 2. Of those that a mesh axis runs over, the one named last changes fastest.
Arguments:
- trailing_cot: bfloat16 [16, 2048, 4, 8192], P(None, 'row', None, 'col'), may hold values from -6 to 6
- panel_factor: bfloat16 [16, 2048, 256], P(None, ('row', 'col')), may hold values from -0.03125 to 0.03125
- panel_cot: bfloat16 [16, 2048, 256], P(None, ('row', 'col')), may hold values from -6 to 6
- block_inverse: float32 [256, 256], replicated, as said below
- row_desc: bfloat16 [16, 2048, 256], P(None, 'row'), may hold values from -6 to 6
- panel_desc: bfloat16 [256, 256], replicated, may hold values from -6 to 6
Outputs:
- adjoint: float32 [16, 2048, 256], P(None, ('row', 'col'))
- diag_cot: float32 [256, 256], replicated
- slope: float32 [2], replicated
Inputs may be any that keep to these rules, and one draw needn't show every extreme that they name: `block_inverse`: lower triangular, diagonal between 0.6 and 1.4.
All inputs are finite; a program needn't handle non-finite values.
Results may differ from a plain program's by a relative error of at most 0.0003.
Values may be sent and summed in bfloat16 or wider, within the bound.
A program may use at most 128 MiB of HBM per device.

v0:
```python
import math

import jax
import jax.numpy as jnp
from jax import lax
from jax.sharding import PartitionSpec as P


def spread(value, axis, source):
    kept = jnp.where(lax.axis_index(axis) == source, value, 0).astype(value.dtype)
    return lax.psum(kept, axis)


def local(trailing_cot, panel_factor, panel_cot, block_inverse, row_desc, panel_desc):
    n_row = lax.axis_size("row")
    n_col = lax.axis_size("col")
    col_pos = lax.axis_index("col")
    tile = block_inverse.shape[0]
    feat = row_desc.shape[2]
    t_rows = trailing_cot.shape[0]
    t_cols = trailing_cot.shape[2]
    thin = tile // n_col
    ratio = n_col // n_row
    offset = col_pos // n_row
    root = col_pos % n_row
    order = t_rows * n_row * tile
    full_rows = lax.all_gather(panel_factor, "col", axis=1, tiled=True)
    every_factor, every_desc = (spread(full_rows, "row", root), spread(row_desc, "row", root))
    col_factor = lax.dynamic_index_in_dim(
        every_factor.reshape(t_cols, ratio, tile, tile), offset, 1, keepdims=False
    )
    col_desc = lax.dynamic_index_in_dim(
        every_desc.reshape(t_cols, ratio, tile, feat), offset, 1, keepdims=False
    )
    product = lax.psum_scatter(
        jnp.einsum("tiuc,ucj->itj", trailing_cot, col_factor, preferred_element_type=jnp.float32),
        "col",
        scatter_dimension=0,
        tiled=True,
    )
    product = jnp.transpose(product, (1, 0, 2))
    total = panel_cot.astype(jnp.float32) - 2.0 * product
    flat_total = total.reshape(-1, tile)
    adjoint = jnp.dot(flat_total, block_inverse, precision=lax.Precision.HIGHEST)
    moment_part = jnp.dot(
        flat_total.T,
        panel_factor.reshape(-1, tile).astype(jnp.float32),
        precision=lax.Precision.HIGHEST,
    )
    row_norm = jnp.sum(jnp.square(row_desc.astype(jnp.float32)), axis=-1)
    col_norm = jnp.sum(jnp.square(col_desc.astype(jnp.float32)), axis=-1)
    cross = jnp.einsum("tif,ucf->tiuc", row_desc, col_desc, preferred_element_type=jnp.float32)
    scaled = 2.0 * (row_norm[:, :, None, None] + col_norm[None, None, :, :] - 2.0 * cross) / feat
    trail_local = jnp.sum(trailing_cot.astype(jnp.float32) * (2.0 * scaled * jnp.exp(-scaled)))
    thin_desc = lax.dynamic_slice_in_dim(row_desc, col_pos * thin, thin, 1).reshape(-1, feat)
    thin_norm = jnp.sum(jnp.square(thin_desc.astype(jnp.float32)), axis=-1)
    panel_norm = jnp.sum(jnp.square(panel_desc.astype(jnp.float32)), axis=-1)
    cross_panel = jnp.dot(thin_desc, panel_desc.T, preferred_element_type=jnp.float32)
    scaled_panel = 2.0 * (thin_norm[:, None] + panel_norm[None, :] - 2.0 * cross_panel) / feat
    panel_local = jnp.sum(adjoint * (2.0 * scaled_panel * jnp.exp(-scaled_panel)))
    local_parts = jnp.stack([trail_local, panel_local])
    moment, summed_parts = lax.psum((moment_part, local_parts), ("row", "col"))
    diag_cot = -jnp.tril(jnp.dot(block_inverse.T, moment, precision=lax.Precision.HIGHEST))
    scales = jnp.array([1.0 / order, 1.0 / math.sqrt(order * tile)], jnp.float32)
    slope = summed_parts * scales
    return (adjoint.reshape(t_rows, thin, tile), diag_cot, slope)


def solution(mesh):
    in_specs = (
        P(None, "row", None, "col"),
        P(None, ("row", "col"), None),
        P(None, ("row", "col"), None),
        P(),
        P(None, "row", None),
        P(),
    )
    out_specs = (P(None, ("row", "col"), None), P(), P())
    return jax.shard_map(local, mesh=mesh, in_specs=in_specs, out_specs=out_specs, check_vma=False)
```

profile of v0, /device:TPU:1, one launch (start us, length us, event | category | flops | bytes accessed | tf_op | source)
XLA Modules:
  0.0 670.8 jit_solution(17940780253290286361)
XLA Ops:
  7.2 0.7 all-gather.2.cloned.1.call-update
  8.0 78.0 %all-gather.2.cloned.1.call-done = bf16[16,256,256]{2,1,0:T(8,128)(2,1)} async-done(((bf16[16,8,256]{2,1,0:T(8,128)(2,1)}), bf16[16,256,256]{2,1,0:T(8,128)(2,1)}) %all-gather.2.cloned.1.call-update) | async-done | bytes 2097168 | tf_op jit(solution)/shard_map/all_gather | solution.py:27
  86.0 0.3 broadcast_select_fusion
  86.3 1.5 copy.28
  87.8 2.4 copy.23
  90.2 80.3 %all-reduce.6.cloned.1.call-done = (bf16[4,4,256,256]{2,3,0,1:T(8,128)(2,1)}, bf16[4,4,256,256]{3,2,0,1:T(8,128)(2,1)}) async-done(((bf16[4,4,256,256]{2,3,0,1:T(8,128)(2,1)}, bf16[4,4,256,256]{3,2,0,1:T(8,128)(2,1)}), (bf16[4,4,256,256]{2,3,0,1:T(8,128)(2,1)}, bf16[4,4,256,256]{3,2,0,1:T(8,128)(2,1)})) %all-reduce.6.cloned.1.call-update) | async-done | bytes 4194320 | tf_op jit(solution)/shard_map/psum | solution.py:11
  170.6 7.9 %fusion.2 = f32[256,16,256]{0,2,1:T(8,128)} fusion(bf16[16,256,4,256]{3,2,1,0:T(4,128)(2,1)} %param.7, bf16[4,4,256,256]{2,3,0,1:T(8,128)(2,1)} %get-tuple-element.12, s32[]{:T(128)S(6)} %select_n.39), kind=kOutput, calls=%fused_computation.5 | convolution fusion | flops 2147483648 | bytes 13107204 | tf_op jit(solution)/shard_map/tiuc,ucj->itj/dot_general | solution.py:36
  178.4 5.4 copy.25
  184.0 13.8 %copy.27 = bf16[16,256,4,256]{1,3,0,2:T(8,128)(2,1)} copy(bf16[16,256,4,256]{3,2,1,0:T(4,128)(2,1)} %param.7) | data formatting | bytes 16777216 | tf_op args[0]
  197.8 0.1 multiply_reduce_fusion.5
  198.0 0.1 multiply_reduce_fusion.3
  198.1 0.6 multiply_reduce_fusion.1
  198.8 1.3 multiply_reduce_fusion.2
  200.1 10.4 %multiply_reduce_fusion = f32[]{:T(128)} fusion(bf16[16,256,4,256]{1,3,0,2:T(8,128)(2,1)} %copy.27, f32[4,256]{1,0:T(4,128)S(1)} %multiply_reduce_fusion.2, f32[16,256]{1,0:T(8,128)S(1)} %multiply_reduce_fusion.1, bf16[16,256,256]{2,1,0:T(8,128)(2,1)S(1)} %copy-done.1, bf16[4,4,256,256]{3,2,0,1:T(8,128)(2,1)} %get-tuple-element.13, s32[]{:T(128)S(6)} %select_n.39), kind=kOutput, calls=%fused_computation.1 | convolution fusion | flops 2189426688 | bytes 11030536 | tf_op jit(solution)/shard_map/tif,ucf->tiuc/dot_general | solution.py:52
  210.4 191.8 %reduce-scatter.2.cloned.1.call-done = f32[8,16,256]{2,1,0:T(8,128)} async-done(((f32[256,16,256]{2,1,0:T(8,128)}), f32[8,16,256]{2,1,0:T(8,128)}) %reduce-scatter.2.cloned.1.call-update) | async-done | bytes 131088 | tf_op jit(solution)/shard_map/reduce_scatter | solution.py:35
  402.3 2.0 convolution_bitcast_fusion.1
  404.3 1.2 fusion.13
  405.5 0.8 multiply_reduce_fusion.4
  406.4 1.3 pad_maximum_fusion
  407.7 79.7 %psum.31 = f32[2]{0:T(128)S(1)} all-reduce(f32[2]{0:T(128)S(1)} %pad_maximum_fusion), channel_id=1, replica_groups=mesh['row'=8,'col'=32] {'row','col'}, use_global_device_ids=true, to_apply=%region_10.11 | all-reduce | flops 2 | bytes 16 | tf_op jit(solution)/shard_map/psum | solution.py:62
  487.4 0.5 mul.63
  487.9 173.9 %all-reduce.4.cloned.1.call-done = f32[256,256]{1,0:T(8,128)} async-done(((f32[256,256]{1,0:T(8,128)}), f32[256,256]{1,0:T(8,128)}) %all-reduce.4.cloned.1.call-update) | async-done | bytes 262160 | tf_op jit(solution)/shard_map/psum | solution.py:62
  661.8 1.5 fusion.7
  663.4 0.8 copy.29
  (22 shorter events, 0.3 us)
Async XLA Ops:
  7.2 397.1 %copy-start = (f32[256,256]{1,0:T(8,128)S(1)}, f32[256,256]{1,0:T(8,128)}, u32[]{:S(2)}) copy-start(f32[256,256]{1,0:T(8,128)} %param.10) | copy-start | bytes 786436
  7.2 78.8 %all-gather.2.cloned.1.call-start = ((), (), s32[]{:S(2)}) async-start(), calls=%async_computation.1 | async-start | bytes 2162688 | tf_op jit(solution)/shard_map/all_gather | solution.py:27
  7.9 162.7 %all-reduce.6.cloned.1.call-start = ((), (), s32[]{:S(2)}) async-start(), calls=%async_computation.4 | async-start | bytes 8388608 | tf_op jit(solution)/shard_map/psum | solution.py:11
  90.2 312.1 %reduce-scatter.2.cloned.1.call-start = ((), (), s32[]{:S(2)}) async-start(), calls=%async_computation.2 | async-start | bytes 4325376 | tf_op jit(solution)/shard_map/reduce_scatter | solution.py:35
  183.9 477.9 %all-reduce.4.cloned.1.call-start = ((), (), s32[]{:S(2)}) async-start(), calls=%async_computation.3 | async-start | bytes 524288 | tf_op jit(solution)/shard_map/psum | solution.py:62
  184.0 13.9 %copy-start.1 = (bf16[16,256,256]{2,1,0:T(8,128)(2,1)S(1)}, bf16[16,256,256]{2,1,0:T(8,128)(2,1)}, u32[]{:S(2)}) copy-start(bf16[16,256,256]{2,1,0:T(8,128)(2,1)} %param.11) | copy-start | bytes 6291460
  184.0 14.0 %copy-start.2 = (bf16[256,256]{1,0:T(8,128)(2,1)S(1)}, bf16[256,256]{1,0:T(8,128)(2,1)}, u32[]{:S(2)}) copy-start(bf16[256,256]{1,0:T(8,128)(2,1)} %param.12) | copy-start | bytes 393220
  200.0 202.2 %copy-start.4 = (bf16[16,8,256]{2,1,0:T(8,128)(2,1)S(1)}, bf16[16,8,256]{2,1,0:T(8,128)(2,1)}, u32[]{:S(2)}) copy-start(bf16[16,8,256]{2,1,0:T(8,128)(2,1)} %param.9) | copy-start | bytes 196612
  200.0 202.2 %copy-start.5 = (bf16[16,8,256]{2,1,0:T(8,128)(2,1)S(1)}, bf16[16,8,256]{2,1,0:T(8,128)(2,1)}, u32[]{:S(2)}) copy-start(bf16[16,8,256]{2,1,0:T(8,128)(2,1)} %param.8) | copy-start | bytes 196612
  200.0 287.4 %copy-start.6 = (f32[2]{0:T(128)S(1)}, f32[2]{0:T(128)}, u32[]{:S(2)}) copy-start(f32[2]{0:T(128)} %constant.69.clone) | copy-start | bytes 28
  405.5 258.7 %copy-start.3 = (f32[128,256]{1,0:T(8,128)}, f32[128,256]{1,0:T(8,128)S(1)}, u32[]{:S(2)}) copy-start(f32[128,256]{1,0:T(8,128)S(1)} %fusion.13) | copy-start | bytes 393220
Sparse Core Ops, SparseCore 0:
  10.5 75.4 all-gather.1
  90.3 80.2 all-reduce.5
  184.0 218.1 reduce-scatter.1
  409.0 252.7 all-reduce.3
where the time goes:
time: 672 us; the launch traced here: 671 us
  waiting for transfers between devices  525 us (78%)
  blocking collectives  79.7 us (12%)
  local copies, waits for them, and re-layouts  24.1 us (4%)
  matrix products  23.8 us (4%)
  between operations  13.9 us (2%)
    reduce_scatter x1, waiting for transfers between devices, local(): lax.psum_scatter(jnp.einsum('tiuc,ucj->itj', trailing_cot, col_factor, pr...  192 us
    psum x1, waiting for transfers between devices, local(): moment, summed_parts = lax.psum((moment_part, local_parts), ('row', 'col'))  174 us
    psum x1, waiting for transfers between devices, spread(): return lax.psum(kept, axis)  80.3 us
    psum x1, blocking collectives, local(): moment, summed_parts = lax.psum((moment_part, local_parts), ('row', 'col'))  79.7 us
    all_gather x1, waiting for transfers between devices, local(): full_rows = lax.all_gather(panel_factor, 'col', axis=1, tiled=True)  78 us
    unnamed x16, local copies, waits for them, and re-layouts  14.7 us
  transfers between devices with their start and end apart: 4, of which 4 were waited for; matrix products, arithmetic and copies ran while one was open for 5% of the time, Pallas kernels for 0%

commit v1 on v0

v1 whole, which is shorter than its diff:
```python
import functools
import math

import jax
import jax.numpy as jnp
from jax import lax
from jax.experimental import pallas as pl
from jax.experimental.pallas import tpu as pltpu
from jax.sharding import PartitionSpec as P

MESH = pl.DeviceIdType.MESH
HIGHEST = lax.Precision.HIGHEST
F32 = jnp.float32
BF16 = jnp.bfloat16
LOG2E = math.log2(math.e)

TR = 16
TC = 4
NX, NY, NZ, NR = 4, 4, 8, 8
PER = 2
KINDS = "ABABABAA"
N_A = KINDS.count("A")
N_B = KINDS.count("B")
STEPS = 7


def kernel(
    f_hbm, u_hbm, s_hbm, c_ref, f_own, b_ref, pd_ref,
    adj_ref, diag_ref, slope_ref,
    s_raw, s_f32, s_rel, u_row, u_col, norm_row, norm_col, f_buf, f_col, prod, total,
    ay1, ay2, az1, az2, bz1, bz2, by1, by2,
    m1, m1r, m2, m2r, m3, m4, m5,
    s_sem, u_sem, f_send, f_recv, f_local, ucol_send, ucol_recv, rs_send, rs_recv, m_send, m_recv,
):
    r = lax.axis_index("row")
    c = lax.axis_index("col")
    x, core = r // 2, r % 2
    z, y = c // NY, c % NY
    root = c % NR
    quarter = c // NR
    is_root = root == r

    barrier = pltpu.get_barrier_semaphore()

    def greet(dev):
        pl.semaphore_signal(barrier, inc=1, device_id=dev, device_id_type=MESH)

    @pl.loop(0, 16)
    def _(m):
        @pl.when(jnp.logical_not(jnp.logical_and(is_root, 2 * m + core == c)))
        def _():
            greet((root, 2 * m + core))

    @pl.loop(1, NR)
    def _(d):
        greet(((r + d) % NR, c))

    @pl.loop(1, NY)
    def _(d):
        greet((r, z * NY + (y + d) % NY))

    @pl.loop(1, NZ)
    def _(d):
        greet((r, ((z + d) % NZ) * NY + y))

    s_copies = [
        pltpu.make_async_copy(s_hbm.at[pl.ds(t * 2048, 2048)], s_raw.at[t], s_sem.at[t])
        for t in range(TR)
    ]
    u_copy = pltpu.make_async_copy(u_hbm, u_row, u_sem)
    for cp in s_copies[:2]:
        cp.start()
    u_copy.start()
    for cp in s_copies[2:]:
        cp.start()

    pl.semaphore_wait(barrier, 16 + 7 + 3 + 7 - jnp.where(is_root, 1, 0))

    @pl.loop(0, 16)
    def _(n):
        q, xd = n // NX, n % NX
        mine = jnp.logical_and(is_root, jnp.logical_and(q == quarter, xd == x))

        @pl.when(mine)
        def _():
            pltpu.make_async_copy(f_hbm.at[q], f_buf.at[c % 2, c // 2], f_recv.at[0]).start()

        @pl.when(jnp.logical_not(mine))
        def _():
            pltpu.make_async_remote_copy(
                src_ref=f_hbm.at[q], dst_ref=f_buf.at[c % 2, c // 2],
                send_sem=f_send.at[n], recv_sem=f_recv.at[0],
                device_id=(2 * xd + c % 2, NR * q + r), device_id_type=MESH,
            ).start()

    def ucol_to(d):
        return pltpu.make_async_remote_copy(
            src_ref=u_hbm.at[:, quarter], dst_ref=u_col,
            send_sem=ucol_send.at[d], recv_sem=ucol_recv,
            device_id=(((x + d) % NX) * 2 + core, c), device_id_type=MESH,
        )

    @pl.when(is_root)
    def _():
        for d in (1, 3, 2):
            ucol_to(d).start()
        pltpu.make_async_copy(u_hbm.at[:, quarter], u_col, ucol_recv).start()

    def relay(t):
        s_f32[...] = s_raw[t].astype(F32)
        for u in range(TC):
            for half in range(2):
                s_rel[t, u, :, half * 128 : half * 128 + 128] = s_f32[
                    pl.ds(half * 4 + u, 256, stride=8), :
                ].astype(BF16)

    for t in range(TR):
        s_copies[t].wait()

    @pl.loop(0, TR)
    def _(t):
        relay(t)

    u_copy.wait()

    @pl.loop(0, TR)
    def _(t):
        rows = u_row[t // 4, t % 4].astype(F32)
        norm = jnp.sum(rows * rows, axis=-1, keepdims=True) * (2.0 * LOG2E / 256.0)
        norm_row[t] = jnp.broadcast_to(norm, (256, 128))

    sibling = (2 * x + 1 - core, c)

    pltpu.make_async_copy(f_buf.at[0], f_buf.at[0], f_recv.at[0]).wait()
    f_swap = pltpu.make_async_remote_copy(
        src_ref=f_buf.at[core], dst_ref=f_buf.at[core],
        send_sem=f_local, recv_sem=f_recv.at[1],
        device_id=sibling, device_id_type=MESH,
    )
    f_swap.start()
    f_swap.wait_recv()

    @pl.loop(0, 16)
    def _(m):
        even = f_buf[0, m].astype(F32)
        odd = f_buf[1, m].astype(F32)
        for u in range(TC):
            rows = jnp.concatenate([even[8 * u : 8 * u + 8], odd[8 * u : 8 * u + 8]], axis=0)
            f_col[u, pl.ds(pl.multiple_of(m * 16, 16), 16), :] = rows.astype(BF16)

    neighbours = {
        "y": ((r, z * NY + (y + 1) % NY), (r, z * NY + (y + NY - 1) % NY)),
        "z": ((r, ((z + 1) % NZ) * NY + y), (r, ((z + NZ - 1) % NZ) * NY + y)),
    }
    size = {"y": NY, "z": NZ}
    here = {"y": y, "z": z}
    lanes = (pl.ds(0, 128), pl.ds(128, 128))
    full = pl.ds(0, 256)
    group_slot = {}
    for g, kind in enumerate(KINDS):
        group_slot[g] = KINDS[:g].count(kind)

    def part(g, axis, dest, lane):
        rows = pl.ds(g * PER, PER)
        if KINDS[g] == "A":
            if axis == "y":
                return (rows, slice(None), dest, slice(None), lane)
            return (rows, dest, y, slice(None), lane)
        if axis == "z":
            return (rows, dest, slice(None), slice(None), lane)
        return (rows, z, dest, slice(None), lane)

    def box(g, axis, rnd, way):
        slot = group_slot[g]
        if KINDS[g] == "A":
            first, later = (ay1, ay2) if axis == "y" else (az1, az2)
        else:
            first, later = (bz1, bz2) if axis == "z" else (by1, by2)
        if rnd == 0:
            return first.at[slot, way]
        return later.at[slot, way, rnd - 1]

    def sem_of(g, axis, rnd, way):
        second = axis == ("z" if KINDS[g] == "A" else "y")
        offset = (size["y"] // 2 if KINDS[g] == "A" else size["z"] // 2) if second else 0
        return (g * 6 + offset + rnd) * 2 + way

    def copy_of(g, axis, rnd, way):
        n = size[axis]
        reach = n // 2 - rnd
        sign = 1 if way == 0 else n - 1
        dest = (here[axis] + sign * reach) % n
        lane = lanes[way] if rnd == 0 else full
        k = sem_of(g, axis, rnd, way)
        return pltpu.make_async_remote_copy(
            src_ref=prod.at[part(g, axis, dest, lane)],
            dst_ref=box(g, axis, rnd, way),
            send_sem=rs_send.at[k], recv_sem=rs_recv.at[k],
            device_id=neighbours[axis][way], device_id_type=MESH,
        )

    def take(g, axis, rnd, way):
        n = size[axis]
        reach = n // 2 - rnd - 1
        sign = 1 if way == 0 else n - 1
        dest = (here[axis] + sign * reach) % n
        lane = lanes[way] if rnd == 0 else full
        copy_of(g, axis, rnd, way).wait_recv()
        at = part(g, axis, dest, lane)
        prod[at] = prod[at] + box(g, axis, rnd, way)[...]

    def product(g):
        for t in range(g * PER, g * PER + PER):
            out = jnp.dot(s_rel[t, 0], f_col[0], preferred_element_type=F32)
            for u in range(1, TC):
                out += jnp.dot(s_rel[t, u], f_col[u], preferred_element_type=F32)
            prod[t] = out.reshape(NZ, NY, 8, 256)

    def step(g, k):
        axes = ("y", "z") if KINDS[g] == "A" else ("z", "y")
        first = size[axes[0]] // 2
        if k == 0:
            product(g)
            for way in range(2):
                copy_of(g, axes[0], 0, way).start()
            return
        for way in range(2):
            if k <= first:
                take(g, axes[0], k - 1, way)
                if k < first:
                    copy_of(g, axes[0], k, way).start()
            else:
                take(g, axes[1], k - first - 1, way)
                if k < STEPS - 1:
                    copy_of(g, axes[1], k - first, way).start()
        if k == first:
            for way in range(2):
                copy_of(g, axes[1], 0, way).start()

    def slope_unit(n, acc):
        t, u = n // TC, n % TC
        cross = lax.dot_general(
            u_row[t // 4, t % 4], u_col[u], (((1,), (1,)), ((), ())), preferred_element_type=F32
        )
        across = norm_col[u]
        for k in range(0, 256, 32):
            down = norm_row[t, k : k + 32]
            norms = jnp.concatenate([down, down], axis=1) + across[0:1]
            minus = cross[k : k + 32] * (4.0 * LOG2E / 256.0) - norms
            term = s_rel[t, u, k : k + 32].astype(F32) * (minus * jnp.exp2(minus))
            acc = acc + jnp.sum(term.reshape(4, 8, 256), axis=0)
        return acc

    def ucol_forward():
        return pltpu.make_async_remote_copy(
            src_ref=u_col, dst_ref=u_col,
            send_sem=ucol_send.at[0], recv_sem=ucol_recv,
            device_id=sibling, device_id_type=MESH,
        )

    step(0, 0)
    step(1, 0)
    pltpu.make_async_copy(u_col, u_col, ucol_recv).wait()

    @pl.when(core == root % 2)
    def _():
        ucol_forward().start()

    step(2, 0)
    step(3, 0)
    for u in range(TC):
        cols = u_col[u].astype(F32)
        norm = lax.dot_general(
            jnp.ones((8, 256), F32), cols * cols, (((1,), (1,)), ((), ())),
            precision=HIGHEST, preferred_element_type=F32,
        )
        norm_col[u] = norm * (2.0 * LOG2E / 256.0)

    n_groups = len(KINDS)
    ticks = n_groups + STEPS - 1
    n_units = TR * TC
    busy = ticks - 2
    acc = jnp.zeros((8, 256), F32)
    done = 0
    for tick in range(1, ticks):
        for g in range(n_groups):
            k = tick - g
            if g < 4 and k <= 0:
                continue
            if 0 <= k < STEPS:
                step(g, k)
        until = min(n_units, (n_units * tick + busy - 1) // busy)
        if until > done:
            acc = lax.fori_loop(done, until, slope_unit, acc)
            done = until
    trail = jnp.sum(acc) * (-2.0 / LOG2E / 32768.0)

    for t in range(TR):
        total[pl.ds(t * 8, 8), :] = (
            c_ref[pl.ds((t // 2) * 16, 16), :].astype(F32)[(t % 2) * 8 : (t % 2) * 8 + 8]
            - 2.0 * prod[t, z, y]
        )
    whole = total[...]
    adjoint = jnp.dot(whole, b_ref[...], precision=HIGHEST, preferred_element_type=F32)
    adj_ref[...] = adjoint
    moment = lax.dot_general(
        whole, f_own[...].astype(F32), (((0,), (0,)), ((), ())),
        precision=HIGHEST, preferred_element_type=F32,
    )
    m1[:, 0:32, :] = moment.reshape(NR, 32, 256)

    panel = pd_ref[...].astype(F32)
    panel_norm = lax.dot_general(
        jnp.ones((8, 256), F32), panel * panel, (((1,), (1,)), ((), ())),
        precision=HIGHEST, preferred_element_type=F32,
    )
    first_row = pl.multiple_of((c // 2) * 16, 16)
    own = []
    for t in range(TR):
        pair = u_row[t // 4, t % 4, pl.ds(first_row, 16), :].astype(F32)
        own.append(jnp.where(c % 2 == 0, pair[0:8], pair[8:16]))
    own = jnp.concatenate(own, axis=0)
    own_norm = jnp.sum(own * own, axis=-1, keepdims=True)
    cross = lax.dot_general(
        own.astype(BF16), pd_ref[...], (((1,), (1,)), ((), ())), preferred_element_type=F32
    )
    scaled = (2.0 / 256.0) * (own_norm + panel_norm[0:1] - 2.0 * cross)
    panel_part = jnp.sum(adjoint * (2.0 * scaled * jnp.exp(-scaled))) * (1.0 / math.sqrt(8388608))
    lane = lax.broadcasted_iota(jnp.int32, (8, 256), 1)
    scalars = jnp.where(lane < 128, trail, panel_part)
    for j in range(NR):
        m1[j, 32:40, :] = scalars

    def exchange(stage, n, me, dev, src, dst):
        base = (0, 8, 12, 20, 24)[stage]

        def copy(d):
            peer = (me + d) % n
            return pltpu.make_async_remote_copy(
                src_ref=src(peer), dst_ref=dst.at[me],
                send_sem=m_send.at[base + d], recv_sem=m_recv.at[base + d],
                device_id=dev(peer), device_id_type=MESH,
            )

        @pl.loop(1, n)
        def _(d):
            copy(d).start()

        @pl.loop(1, n)
        def _(d):
            copy(d).wait()

    row_dev = lambda p: (p, c)
    y_dev = lambda p: (r, z * NY + p)
    z_dev = lambda p: (r, p * NY + y)

    m1r[r] = m1[r]
    exchange(0, NR, r, row_dev, lambda p: m1.at[p], m1r)
    part1 = m1r[0]
    for j in range(1, NR):
        part1 = part1 + m1r[j]
    for j in range(NY):
        m2[j, 0:8] = part1[8 * j : 8 * j + 8]
        m2[j, 8:16] = part1[32:40]
    m2r[y] = m2[y]
    exchange(1, NY, y, y_dev, lambda p: m2.at[p], m2r)
    m3[z] = ((m2r[0] + m2r[1]) + m2r[2]) + m2r[3]
    exchange(2, NZ, z, z_dev, lambda p: m3.at[z], m3)
    part3 = m3[0]
    for j in range(1, NZ):
        part3 = part3 + m3[j]
    m4[y] = part3[0:8]
    exchange(3, NY, y, y_dev, lambda p: m4.at[y], m4)
    m5[r] = m4[...].reshape(32, 256)
    exchange(4, NR, r, row_dev, lambda p: m5.at[r], m5)
    diag = lax.dot_general(
        b_ref[...], m5[...].reshape(256, 256), (((0,), (0,)), ((), ())),
        precision=HIGHEST, preferred_element_type=F32,
    )
    down = lax.broadcasted_iota(jnp.int32, (256, 256), 0)
    across = lax.broadcasted_iota(jnp.int32, (256, 256), 1)
    diag_ref[...] = jnp.where(down >= across, -diag, 0.0)
    slope_ref[...] = jnp.concatenate([part3[8:9, 0:1], part3[8:9, 128:129]], axis=1)

    @pl.loop(0, 16)
    def _(n):
        q, xd = n // NX, n % NX
        mine = jnp.logical_and(is_root, jnp.logical_and(q == quarter, xd == x))

        @pl.when(jnp.logical_not(mine))
        def _():
            pltpu.make_async_remote_copy(
                src_ref=f_hbm.at[q], dst_ref=f_buf.at[c % 2, c // 2],
                send_sem=f_send.at[n], recv_sem=f_recv.at[0],
                device_id=(2 * xd + c % 2, NR * q + r), device_id_type=MESH,
            ).wait_send()

    @pl.when(is_root)
    def _():
        for d in (1, 2, 3):
            ucol_to(d).wait_send()

    @pl.when(core == root % 2)
    def _():
        ucol_forward().wait_send()

    f_swap.wait_send()
    for g, kind in enumerate(KINDS):
        for axis in "yz":
            for rnd in range(size[axis] // 2):
                for way in range(2):
                    copy_of(g, axis, rnd, way).wait_send()


def local(trailing_cot, panel_factor, panel_cot, block_inverse, row_desc, panel_desc):
    s_rows = trailing_cot.reshape(TR, 256, TC, 2, 128).transpose(0, 1, 3, 2, 4).reshape(TR * 2048, 128)
    f_parts = panel_factor.reshape(4, 4, 8, 256).transpose(1, 0, 2, 3).reshape(4, 32, 256)
    hbm = pl.BlockSpec(memory_space=pl.ANY)
    vmem = pl.BlockSpec(memory_space=pltpu.VMEM)
    dma = pltpu.SemaphoreType.DMA
    V = pltpu.VMEM
    adjoint, diag, slope = pl.pallas_call(
        kernel,
        out_shape=(
            jax.ShapeDtypeStruct((128, 256), F32),
            jax.ShapeDtypeStruct((256, 256), F32),
            jax.ShapeDtypeStruct((1, 2), F32),
        ),
        in_specs=[hbm, hbm, hbm, vmem, vmem, vmem, vmem],
        out_specs=(vmem, vmem, vmem),
        scratch_shapes=[
            V((TR, 2048, 128), BF16),
            V((2048, 128), F32),
            V((TR, TC, 256, 256), BF16),
            V((4, 4, 256, 256), BF16),
            V((TC, 256, 256), BF16),
            V((TR, 256, 128), F32),
            V((TC, 8, 256), F32),
            V((2, 16, 32, 256), BF16),
            V((TC, 256, 256), BF16),
            V((TR, NZ, NY, 8, 256), F32),
            V((128, 256), F32),
            V((N_A, 2, PER, NZ, 8, 128), F32),
            V((N_A, 2, 1, PER, NZ, 8, 256), F32),
            V((N_A, 2, PER, 8, 128), F32),
            V((N_A, 2, 3, PER, 8, 256), F32),
            V((N_B, 2, PER, NY, 8, 128), F32),
            V((N_B, 2, 3, PER, NY, 8, 256), F32),
            V((N_B, 2, PER, 8, 128), F32),
            V((N_B, 2, 1, PER, 8, 256), F32),
            V((NR, 40, 256), F32),
            V((NR, 40, 256), F32),
            V((NY, 16, 256), F32),
            V((NY, 16, 256), F32),
            V((NZ, 16, 256), F32),
            V((NY, 8, 256), F32),
            V((NR, 32, 256), F32),
            dma((TR,)),
            dma,
            dma((16,)),
            dma((2,)),
            dma,
            dma((4,)),
            dma,
            dma((len(KINDS) * 12,)),
            dma((len(KINDS) * 12,)),
            dma((32,)),
            dma((32,)),
        ],
        compiler_params=pltpu.CompilerParams(
            collective_id=0, has_side_effects=True, vmem_limit_bytes=60 * 1024 * 1024
        ),
        cost_estimate=pl.CostEstimate(
            flops=4 * 4096 * 1024 * 256, bytes_accessed=12 * 1024 * 1024, transcendentals=4096 * 1024
        ),
        name="panel_step",
    )(
        f_parts,
        row_desc.reshape(4, 4, 256, 256),
        s_rows,
        panel_cot.reshape(128, 256),
        panel_factor.reshape(128, 256),
        block_inverse,
        panel_desc,
    )
    return adjoint.reshape(16, 8, 256), diag, slope.reshape(2)


def solution(mesh):
    in_specs = (
        P(None, "row", None, "col"),
        P(None, ("row", "col"), None),
        P(None, ("row", "col"), None),
        P(),
        P(None, "row", None),
        P(),
    )
    out_specs = (P(None, ("row", "col"), None), P(), P())
    return jax.shard_map(local, mesh=mesh, in_specs=in_specs, out_specs=out_specs, check_vma=False)
```

time: 672 us -> 121 us (0.18)
  waiting for transfers between devices: 525 us -> 0 us
  Pallas kernels: 0 us -> 114 us
  blocking collectives: 79.7 us -> 0 us
  matrix products: 23.8 us -> 0 us
  local copies, waits for them, and re-layouts: 24.1 us -> 5.83 us
  between operations: 13.9 us -> 0.64 us
    psum x2 -> x0, waiting for transfers between devices: 254 us -> none  [the longest x1 174 us: local(): moment, summed_parts = lax.psum((moment_part, local_parts), ('row', 'col'))]
    reduce_scatter x1 -> x0, waiting for transfers between devices: 192 us -> none  [local(): lax.psum_scatter(jnp.einsum('tiuc,ucj->itj', trailing_cot, col_factor, pr...]
    pallas_call x0 -> x1, Pallas kernels: none -> 114 us  [local(): pl.pallas_call(kernel, out_shape=(jax.ShapeDtypeStruct((128, 256), F32),...]
    psum x1 -> x0, blocking collectives: 79.7 us -> none  [local(): moment, summed_parts = lax.psum((moment_part, local_parts), ('row', 'col'))]
    all_gather x1 -> x0, waiting for transfers between devices: 78 us -> none  [local(): full_rows = lax.all_gather(panel_factor, 'col', axis=1, tiled=True)]
    dot_general x6 -> x0, matrix products: 23.8 us -> none  [the longest x1 10.4 us: local(): jnp.einsum('tif,ucf->tiuc', row_desc, col_desc, preferred_element_type=jn...]
    unnamed x16 -> x3, local copies, waits for them, and re-layouts: 14.7 us -> 4.35 us
  transfers between devices with their start and end apart: 4 -> 0, of which waited for: 4 -> 0; matrix products, arithmetic and copies ran while one was open for 5% -> 0% of each run, Pallas kernels for 0% -> 0%
where the time goes in v1:
time: 121 us
  Pallas kernels  114 us (94%)
  local copies, waits for them, and re-layouts  5.83 us (5%)
    pallas_call x1, Pallas kernels, local(): pl.pallas_call(kernel, out_shape=(jax.ShapeDtypeStruct((128, 256), F32),...  114 us
    unnamed x3, local copies, waits for them, and re-layouts  4.35 us

profile of v1, /device:TPU:1, one launch (start us, length us, event | category | flops | bytes accessed | tf_op | source)
XLA Modules:
  0.0 120.8 jit_solution(7798629540270172359)
XLA Ops:
  0.6 1.5 %copy.12 = bf16[4,4,8,256]{3,2,0,1:T(8,128)(2,1)} copy(bf16[4,4,8,256]{3,2,1,0:T(8,128)(2,1)} %bitcast.17) | data formatting | bytes 131072 | tf_op jit(solution)/shard_map/reshape | solution.py:417
  2.1 114.3 %panel_step.1 = (f32[128,256]{1,0:T(8,128)}, f32[256,256]{1,0:T(8,128)}, f32[1,2]{1,0:T(1,128)}) custom-call(bf16[4,32,256]{2,1,0:T(8,128)(2,1)} %bitcast.19, bf16[4,4,256,256]{3,2,1,0:T(8,128)(2,1)} %bitcast.21, bf16[32768,128]{1,0:T(8,128)(2,1)} %bitcast.20, bf16[128,256]{1,0:T(8,128)(2,1)} %bitcast.22, bf16[128,256]{1,0:T(8,128)(2,1)} %bitcast.18, ...), custom_call_target="tpu_custom_call" | custom-call | flops 4294967296 | bytes 12582912 | tf_op jit(solution)/shard_map/panel_step/pallas_call | solution.py:422
  116.5 1.6 %copy.16 = f32[16,8,256]{2,1,0:T(8,128)} copy(f32[16,8,256]{2,1,0:T(8,128)} %bitcast.16) | data formatting | bytes 262144
  118.0 1.7 %copy.17 = f32[256,256]{1,0:T(8,128)} copy(f32[256,256]{1,0:T(8,128)} %get-tuple-element.13) | data formatting | bytes 524288
  119.7 1.1 copy.18

commit v2 on v1

--- a/solution.py
+++ b/solution.py
@@ -25,11 +25,11 @@
 
 
 def kernel(
-    f_hbm, u_hbm, s_hbm, c_ref, f_own, b_ref, pd_ref,
+    u_hbm, s_hbm, c_ref, f_own, b_ref, pd_ref,
     adj_ref, diag_ref, slope_ref,
-    s_raw, s_f32, s_rel, u_row, u_col, norm_row, norm_col, f_buf, f_col, prod, total,
+    s_raw, s_f32, s_rel, u_row, u_col, norm_row, norm_col, f_parts, f_buf, f_col, prod, total, near,
     ay1, ay2, az1, az2, bz1, bz2, by1, by2,
-    m1, m1r, m2, m2r, m3, m4, m5,
+    m1, m1r, m3, m5,
     s_sem, u_sem, f_send, f_recv, f_local, ucol_send, ucol_recv, rs_send, rs_recv, m_send, m_recv,
 ):
     r = lax.axis_index("row")
@@ -39,6 +39,15 @@
     root = c % NR
     quarter = c // NR
     is_root = root == r
+    feeds = core == y % 2
+    place = r * NY + y
+
+    def near_dev(p):
+        return (p // NY, z * NY + p % NY)
+
+    def partner(u):
+        side = z + 1 - 2 * (z % 2) if u // 2 else z
+        return side * NY + (y + 2 * (u % 2)) % NY
 
     barrier = pltpu.get_barrier_semaphore()
 
@@ -51,17 +60,18 @@
         def _():
             greet((root, 2 * m + core))
 
-    @pl.loop(1, NR)
+    @pl.loop(1, NR * NY)
     def _(d):
-        greet(((r + d) % NR, c))
-
-    @pl.loop(1, NY)
-    def _(d):
-        greet((r, z * NY + (y + d) % NY))
+        greet(near_dev((place + d) % (NR * NY)))
 
     @pl.loop(1, NZ)
     def _(d):
         greet((r, ((z + d) % NZ) * NY + y))
+
+    @pl.when(jnp.logical_and(feeds, jnp.logical_not(is_root)))
+    def _():
+        for u in range(TC):
+            greet((root, partner(u)))
 
     s_copies = [
         pltpu.make_async_copy(s_hbm.at[pl.ds(t * 2048, 2048)], s_raw.at[t], s_sem.at[t])
@@ -74,7 +84,13 @@
     for cp in s_copies[2:]:
         cp.start()
 
-    pl.semaphore_wait(barrier, 16 + 7 + 3 + 7 - jnp.where(is_root, 1, 0))
+    f_wide = f_own[...].astype(F32)
+    for q in range(4):
+        f_parts[q] = jnp.concatenate(
+            [f_wide[(4 * u + q) * 8 : (4 * u + q) * 8 + 8] for u in range(TC)], axis=0
+        ).astype(BF16)
+
+    pl.semaphore_wait(barrier, 16 + 31 + 7 - jnp.where(is_root, 1, 0) + jnp.where(feeds, 3, 0))
 
     @pl.loop(0, 16)
     def _(n):
@@ -83,27 +99,31 @@
 
         @pl.when(mine)
         def _():
-            pltpu.make_async_copy(f_hbm.at[q], f_buf.at[c % 2, c // 2], f_recv.at[0]).start()
+            pltpu.make_async_copy(f_parts.at[q], f_buf.at[c % 2, c // 2], f_recv.at[0]).start()
 
         @pl.when(jnp.logical_not(mine))
         def _():
             pltpu.make_async_remote_copy(
-                src_ref=f_hbm.at[q], dst_ref=f_buf.at[c % 2, c // 2],
+                src_ref=f_parts.at[q], dst_ref=f_buf.at[c % 2, c // 2],
                 send_sem=f_send.at[n], recv_sem=f_recv.at[0],
                 device_id=(2 * xd + c % 2, NR * q + r), device_id_type=MESH,
             ).start()
 
-    def ucol_to(d):
+    def ucol_to(u, d):
         return pltpu.make_async_remote_copy(
-            src_ref=u_hbm.at[:, quarter], dst_ref=u_col,
+            src_ref=u_hbm.at[u, quarter], dst_ref=u_col.at[u],
             send_sem=ucol_send.at[d], recv_sem=ucol_recv,
-            device_id=(((x + d) % NX) * 2 + core, c), device_id_type=MESH,
-        )
+            device_id=(((x + d) % NX) * 2 + core, partner(u)), device_id_type=MESH,
+        )
+
+    for u in range(TC):
+        @pl.when(partner(u) % NR == r)
+        def _():
+            for d in (2, 1, 3):
+                ucol_to(u, d).start()
 
     @pl.when(is_root)
     def _():
-        for d in (1, 3, 2):
-            ucol_to(d).start()
         pltpu.make_async_copy(u_hbm.at[:, quarter], u_col, ucol_recv).start()
 
     def relay(t):
@@ -131,6 +151,19 @@
 
     sibling = (2 * x + 1 - core, c)
 
+    def ucol_forward():
+        return pltpu.make_async_remote_copy(
+            src_ref=u_col, dst_ref=u_col,
+            send_sem=ucol_send.at[0], recv_sem=ucol_recv,
+            device_id=sibling, device_id_type=MESH,
+        )
+
+    pltpu.make_async_copy(u_col, u_col, ucol_recv).wait()
+
+    @pl.when(feeds)
+    def _():
+        ucol_forward().start()
+
     pltpu.make_async_copy(f_buf.at[0], f_buf.at[0], f_recv.at[0]).wait()
     f_swap = pltpu.make_async_remote_copy(
         src_ref=f_buf.at[core], dst_ref=f_buf.at[core],
@@ -138,6 +171,33 @@
         device_id=sibling, device_id_type=MESH,
     )
     f_swap.start()
+
+    for u in range(TC):
+        cols = u_col[u].astype(F32)
+        norm = lax.dot_general(
+            jnp.ones((8, 256), F32), cols * cols, (((1,), (1,)), ((), ())),
+            precision=HIGHEST, preferred_element_type=F32,
+        )
+        norm_col[u] = norm * (2.0 * LOG2E / 256.0)
+
+    panel = pd_ref[...].astype(F32)
+    panel_norm = lax.dot_general(
+        jnp.ones((8, 256), F32), panel * panel, (((1,), (1,)), ((), ())),
+        precision=HIGHEST, preferred_element_type=F32,
+    )
+    first_row = pl.multiple_of((c // 2) * 16, 16)
+    own = []
+    for t in range(TR):
+        pair = u_row[t // 4, t % 4, pl.ds(first_row, 16), :].astype(F32)
+        own.append(jnp.where(c % 2 == 0, pair[0:8], pair[8:16]))
+    own = jnp.concatenate(own, axis=0)
+    own_norm = jnp.sum(own * own, axis=-1, keepdims=True)
+    cross = lax.dot_general(
+        own.astype(BF16), pd_ref[...], (((1,), (1,)), ((), ())), preferred_element_type=F32
+    )
+    scaled = (2.0 / 256.0) * (own_norm + panel_norm[0:1] - 2.0 * cross)
+    near[...] = 2.0 * scaled * jnp.exp(-scaled) * (1.0 / math.sqrt(8388608))
+
     f_swap.wait_recv()
 
     @pl.loop(0, 16)
@@ -251,48 +311,20 @@
             acc = acc + jnp.sum(term.reshape(4, 8, 256), axis=0)
         return acc
 
-    def ucol_forward():
-        return pltpu.make_async_remote_copy(
-            src_ref=u_col, dst_ref=u_col,
-            send_sem=ucol_send.at[0], recv_sem=ucol_recv,
-            device_id=sibling, device_id_type=MESH,
-        )
-
-    step(0, 0)
-    step(1, 0)
-    pltpu.make_async_copy(u_col, u_col, ucol_recv).wait()
-
-    @pl.when(core == root % 2)
-    def _():
-        ucol_forward().start()
-
-    step(2, 0)
-    step(3, 0)
-    for u in range(TC):
-        cols = u_col[u].astype(F32)
-        norm = lax.dot_general(
-            jnp.ones((8, 256), F32), cols * cols, (((1,), (1,)), ((), ())),
-            precision=HIGHEST, preferred_element_type=F32,
-        )
-        norm_col[u] = norm * (2.0 * LOG2E / 256.0)
-
     n_groups = len(KINDS)
-    ticks = n_groups + STEPS - 1
     n_units = TR * TC
-    busy = ticks - 2
     acc = jnp.zeros((8, 256), F32)
     done = 0
-    for tick in range(1, ticks):
-        for g in range(n_groups):
-            k = tick - g
-            if g < 4 and k <= 0:
-                continue
-            if 0 <= k < STEPS:
-                step(g, k)
-        until = min(n_units, (n_units * tick + busy - 1) // busy)
+    for g in range(n_groups):
+        step(g, 0)
+    visits = (STEPS - 1) * n_groups
+    busy = visits - 4
+    for visit in range(visits):
+        until = min(n_units, n_units * (visit + 1) // busy)
         if until > done:
             acc = lax.fori_loop(done, until, slope_unit, acc)
             done = until
+        step(visit % n_groups, 1 + visit // n_groups)
     trail = jnp.sum(acc) * (-2.0 / LOG2E / 32768.0)
 
     for t in range(TR):
@@ -307,33 +339,14 @@
         whole, f_own[...].astype(F32), (((0,), (0,)), ((), ())),
         precision=HIGHEST, preferred_element_type=F32,
     )
-    m1[:, 0:32, :] = moment.reshape(NR, 32, 256)
-
-    panel = pd_ref[...].astype(F32)
-    panel_norm = lax.dot_general(
-        jnp.ones((8, 256), F32), panel * panel, (((1,), (1,)), ((), ())),
-        precision=HIGHEST, preferred_element_type=F32,
-    )
-    first_row = pl.multiple_of((c // 2) * 16, 16)
-    own = []
-    for t in range(TR):
-        pair = u_row[t // 4, t % 4, pl.ds(first_row, 16), :].astype(F32)
-        own.append(jnp.where(c % 2 == 0, pair[0:8], pair[8:16]))
-    own = jnp.concatenate(own, axis=0)
-    own_norm = jnp.sum(own * own, axis=-1, keepdims=True)
-    cross = lax.dot_general(
-        own.astype(BF16), pd_ref[...], (((1,), (1,)), ((), ())), preferred_element_type=F32
-    )
-    scaled = (2.0 / 256.0) * (own_norm + panel_norm[0:1] - 2.0 * cross)
-    panel_part = jnp.sum(adjoint * (2.0 * scaled * jnp.exp(-scaled))) * (1.0 / math.sqrt(8388608))
+    panel_part = jnp.sum(adjoint * near[...])
     lane = lax.broadcasted_iota(jnp.int32, (8, 256), 1)
-    scalars = jnp.where(lane < 128, trail, panel_part)
-    for j in range(NR):
-        m1[j, 32:40, :] = scalars
-
-    def exchange(stage, n, me, dev, src, dst):
-        base = (0, 8, 12, 20, 24)[stage]
-
+    down = lax.broadcasted_iota(jnp.int32, (8, 256), 0)
+    for p in range(NR * NY):
+        block = jnp.where(jnp.logical_and(down == 0, lane == 254), trail, moment[8 * p : 8 * p + 8])
+        m1[p] = jnp.where(jnp.logical_and(down == 0, lane == 255), panel_part, block)
+
+    def exchange(base, n, me, dev, src, dst):
         def copy(d):
             peer = (me + d) % n
             return pltpu.make_async_remote_copy(
@@ -350,29 +363,18 @@
         def _(d):
             copy(d).wait()
 
-    row_dev = lambda p: (p, c)
-    y_dev = lambda p: (r, z * NY + p)
-    z_dev = lambda p: (r, p * NY + y)
-
-    m1r[r] = m1[r]
-    exchange(0, NR, r, row_dev, lambda p: m1.at[p], m1r)
+    m1r[place] = m1[place]
+    exchange(0, NR * NY, place, near_dev, lambda p: m1.at[p], m1r)
     part1 = m1r[0]
-    for j in range(1, NR):
+    for j in range(1, NR * NY):
         part1 = part1 + m1r[j]
-    for j in range(NY):
-        m2[j, 0:8] = part1[8 * j : 8 * j + 8]
-        m2[j, 8:16] = part1[32:40]
-    m2r[y] = m2[y]
-    exchange(1, NY, y, y_dev, lambda p: m2.at[p], m2r)
-    m3[z] = ((m2r[0] + m2r[1]) + m2r[2]) + m2r[3]
-    exchange(2, NZ, z, z_dev, lambda p: m3.at[z], m3)
+    m3[z] = part1
+    exchange(32, NZ, z, lambda p: (r, p * NY + y), lambda p: m3.at[z], m3)
     part3 = m3[0]
     for j in range(1, NZ):
         part3 = part3 + m3[j]
-    m4[y] = part3[0:8]
-    exchange(3, NY, y, y_dev, lambda p: m4.at[y], m4)
-    m5[r] = m4[...].reshape(32, 256)
-    exchange(4, NR, r, row_dev, lambda p: m5.at[r], m5)
+    m5[place] = part3
+    exchange(40, NR * NY, place, near_dev, lambda p: m5.at[place], m5)
     diag = lax.dot_general(
         b_ref[...], m5[...].reshape(256, 256), (((0,), (0,)), ((), ())),
         precision=HIGHEST, preferred_element_type=F32,
@@ -380,7 +382,7 @@
     down = lax.broadcasted_iota(jnp.int32, (256, 256), 0)
     across = lax.broadcasted_iota(jnp.int32, (256, 256), 1)
     diag_ref[...] = jnp.where(down >= across, -diag, 0.0)
-    slope_ref[...] = jnp.concatenate([part3[8:9, 0:1], part3[8:9, 128:129]], axis=1)
+    slope_ref[...] = part3[0:1, 254:256]
 
     @pl.loop(0, 16)
     def _(n):
@@ -390,18 +392,15 @@
         @pl.when(jnp.logical_not(mine))
         def _():
             pltpu.make_async_remote_copy(
-                src_ref=f_hbm.at[q], dst_ref=f_buf.at[c % 2, c // 2],
+                src_ref=f_parts.at[q], dst_ref=f_buf.at[c % 2, c // 2],
                 send_sem=f_send.at[n], recv_sem=f_recv.at[0],
                 device_id=(2 * xd + c % 2, NR * q + r), device_id_type=MESH,
             ).wait_send()
 
-    @pl.when(is_root)
+    @pl.when(feeds)
     def _():
         for d in (1, 2, 3):
-            ucol_to(d).wait_send()
-
-    @pl.when(core == root % 2)
-    def _():
+            ucol_to(0, d).wait_send()
         ucol_forward().wait_send()
 
     f_swap.wait_send()
@@ -414,7 +413,6 @@
 
 def local(trailing_cot, panel_factor, panel_cot, block_inverse, row_desc, panel_desc):
     s_rows = trailing_cot.reshape(TR, 256, TC, 2, 128).transpose(0, 1, 3, 2, 4).reshape(TR * 2048, 128)
-    f_parts = panel_factor.reshape(4, 4, 8, 256).transpose(1, 0, 2, 3).reshape(4, 32, 256)
     hbm = pl.BlockSpec(memory_space=pl.ANY)
     vmem = pl.BlockSpec(memory_space=pltpu.VMEM)
     dma = pltpu.SemaphoreType.DMA
@@ -426,7 +424,7 @@
             jax.ShapeDtypeStruct((256, 256), F32),
             jax.ShapeDtypeStruct((1, 2), F32),
         ),
-        in_specs=[hbm, hbm, hbm, vmem, vmem, vmem, vmem],
+        in_specs=[hbm, hbm, vmem, vmem, vmem, vmem],
         out_specs=(vmem, vmem, vmem),
         scratch_shapes=[
             V((TR, 2048, 128), BF16),
@@ -436,9 +434,11 @@
             V((TC, 256, 256), BF16),
             V((TR, 256, 128), F32),
             V((TC, 8, 256), F32),
+            V((4, 32, 256), BF16),
             V((2, 16, 32, 256), BF16),
             V((TC, 256, 256), BF16),
             V((TR, NZ, NY, 8, 256), F32),
+            V((128, 256), F32),
             V((128, 256), F32),
             V((N_A, 2, PER, NZ, 8, 128), F32),
             V((N_A, 2, 1, PER, NZ, 8, 256), F32),
@@ -448,13 +448,10 @@
             V((N_B, 2, 3, PER, NY, 8, 256), F32),
             V((N_B, 2, PER, 8, 128), F32),
             V((N_B, 2, 1, PER, 8, 256), F32),
-            V((NR, 40, 256), F32),
-            V((NR, 40, 256), F32),
-            V((NY, 16, 256), F32),
-            V((NY, 16, 256), F32),
-            V((NZ, 16, 256), F32),
-            V((NY, 8, 256), F32),
-            V((NR, 32, 256), F32),
+            V((NR * NY, 8, 256), F32),
+            V((NR * NY, 8, 256), F32),
+            V((NZ, 8, 256), F32),
+            V((NR * NY, 8, 256), F32),
             dma((TR,)),
             dma,
             dma((16,)),
@@ -464,8 +461,8 @@
             dma,
             dma((len(KINDS) * 12,)),
             dma((len(KINDS) * 12,)),
-            dma((32,)),
-            dma((32,)),
+            dma((72,)),
+            dma((72,)),
         ],
         compiler_params=pltpu.CompilerParams(
             collective_id=0, has_side_effects=True, vmem_limit_bytes=60 * 1024 * 1024
@@ -475,7 +472,6 @@
         ),
         name="panel_step",
     )(
-        f_parts,
         row_desc.reshape(4, 4, 256, 256),
         s_rows,
         panel_cot.reshape(128, 256),

time: 121 us -> 98.6 us (0.81)
  Pallas kernels: 114 us -> 93.5 us
  local copies, waits for them, and re-layouts: 5.83 us -> 4.35 us
    pallas_call x1, Pallas kernels: 114 us -> 93.5 us  [local(): pl.pallas_call(kernel, out_shape=(jax.ShapeDtypeStruct((128, 256), F32),...]
    reshape x1 -> x0, local copies, waits for them, and re-layouts: 1.47 us -> none  [local(): panel_factor.reshape(4, 4, 8, 256).transpose(1, 0, 2, 3).reshape(4, 32, 256)]
where the time goes in v2:
time: 98.6 us; the launch traced here: 98.5 us
  Pallas kernels  93.5 us (95%)
  local copies, waits for them, and re-layouts  4.35 us (4%)
    pallas_call x1, Pallas kernels, local(): pl.pallas_call(kernel, out_shape=(jax.ShapeDtypeStruct((128, 256), F32),...  93.5 us
    unnamed x3, local copies, waits for them, and re-layouts  4.35 us

profile of v2, /device:TPU:1, one launch (start us, length us, event | category | flops | bytes accessed | tf_op | source)
XLA Modules:
  0.0 98.5 jit_solution(1509539507248926231)
XLA Ops:
  0.6 93.5 %panel_step.1 = (f32[128,256]{1,0:T(8,128)}, f32[256,256]{1,0:T(8,128)}, f32[1,2]{1,0:T(1,128)}) custom-call(bf16[4,4,256,256]{3,2,1,0:T(8,128)(2,1)} %bitcast.12, bf16[32768,128]{1,0:T(8,128)(2,1)} %bitcast.11, bf16[128,256]{1,0:T(8,128)(2,1)} %bitcast.13, bf16[128,256]{1,0:T(8,128)(2,1)} %bitcast.14, f32[256,256]{1,0:T(8,128)} %b_ref.1, ...), custom_call_target="tpu_custom_call" | custom-call | flops 4294967296 | bytes 12582912 | tf_op jit(solution)/shard_map/panel_step/pallas_call | solution.py:420
  94.1 1.6 %copy.13 = f32[16,8,256]{2,1,0:T(8,128)} copy(f32[16,8,256]{2,1,0:T(8,128)} %bitcast.10) | data formatting | bytes 262144
  95.7 1.7 %copy.14 = f32[256,256]{1,0:T(8,128)} copy(f32[256,256]{1,0:T(8,128)} %get-tuple-element.13) | data formatting | bytes 524288
  97.4 1.1 %copy.15 = f32[2]{0:T(128)} copy(f32[2]{0:T(128)} %bitcast.15) | data formatting | bytes 16

commit v3 on v2

--- a/solution.py
+++ b/solution.py
@@ -18,19 +18,20 @@
 TC = 4
 NX, NY, NZ, NR = 4, 4, 8, 8
 PER = 2
-KINDS = "ABABABAA"
+KINDS = "ABABABAB"
 N_A = KINDS.count("A")
 N_B = KINDS.count("B")
+EARLY = 6
 STEPS = 7
 
 
 def kernel(
     u_hbm, s_hbm, c_ref, f_own, b_ref, pd_ref,
-    adj_ref, diag_ref, slope_ref,
-    s_raw, s_f32, s_rel, u_row, u_col, norm_row, norm_col, f_parts, f_buf, f_col, prod, total, near,
+    adj_ref, moment_ref, slope_ref,
+    s_raw, s_f32, s_rel, u_row, u_col, norm_row, norm_col, f_parts, f_buf, f_col, f_z, f_y, prod, total, near_a, near_b, mt, pan,
     ay1, ay2, az1, az2, bz1, bz2, by1, by2,
     m1, m1r, m3, m5,
-    s_sem, u_sem, f_send, f_recv, f_local, ucol_send, ucol_recv, rs_send, rs_recv, m_send, m_recv,
+    s_sem, u_sem, f_send, f_recv, f_local, fz_send, fz_recv, ucol_send, ucol_recv, rs_send, rs_recv, m_send, m_recv,
 ):
     r = lax.axis_index("row")
     c = lax.axis_index("col")
@@ -90,6 +91,25 @@
             [f_wide[(4 * u + q) * 8 : (4 * u + q) * 8 + 8] for u in range(TC)], axis=0
         ).astype(BF16)
 
+    for kind, store in (("A", f_z.at[z]), ("B", f_y.at[y])):
+        for slot, g in enumerate(n for n, k in enumerate(KINDS) if k == kind):
+            store[slot * 16 : slot * 16 + 16, :] = f_own[g * 16 : g * 16 + 16, :]
+
+    def relay(t):
+        s_f32[...] = s_raw[t].astype(F32)
+        for u in range(TC):
+            for half in range(2):
+                s_rel[t, u, :, half * 128 : half * 128 + 128] = s_f32[
+                    pl.ds(half * 4 + u, 256, stride=8), :
+                ].astype(BF16)
+
+    for t in range(EARLY):
+        s_copies[t].wait()
+
+    @pl.loop(0, EARLY)
+    def _(t):
+        relay(t)
+
     pl.semaphore_wait(barrier, 16 + 31 + 7 - jnp.where(is_root, 1, 0) + jnp.where(feeds, 3, 0))
 
     @pl.loop(0, 16)
@@ -126,18 +146,32 @@
     def _():
         pltpu.make_async_copy(u_hbm.at[:, quarter], u_col, ucol_recv).start()
 
-    def relay(t):
-        s_f32[...] = s_raw[t].astype(F32)
-        for u in range(TC):
-            for half in range(2):
-                s_rel[t, u, :, half * 128 : half * 128 + 128] = s_f32[
-                    pl.ds(half * 4 + u, 256, stride=8), :
-                ].astype(BF16)
-
-    for t in range(TR):
+    def fz_to(d):
+        return pltpu.make_async_remote_copy(
+            src_ref=f_z.at[z], dst_ref=f_z.at[z],
+            send_sem=fz_send.at[d], recv_sem=fz_recv.at[d],
+            device_id=(r, ((z + d) % NZ) * NY + y), device_id_type=MESH,
+        )
+
+    def fy_to(d):
+        return pltpu.make_async_remote_copy(
+            src_ref=f_y.at[y], dst_ref=f_y.at[y],
+            send_sem=fz_send.at[NZ + d], recv_sem=fz_recv.at[NZ + d],
+            device_id=(r, z * NY + (y + d) % NY), device_id_type=MESH,
+        )
+
+    @pl.loop(1, NZ)
+    def _(d):
+        fz_to(d).start()
+
+    @pl.loop(1, NY)
+    def _(d):
+        fy_to(d).start()
+
+    for t in range(EARLY, TR):
         s_copies[t].wait()
 
-    @pl.loop(0, TR)
+    @pl.loop(EARLY, TR)
     def _(t):
         relay(t)
 
@@ -149,20 +183,56 @@
         norm = jnp.sum(rows * rows, axis=-1, keepdims=True) * (2.0 * LOG2E / 256.0)
         norm_row[t] = jnp.broadcast_to(norm, (256, 128))
 
+    panel = pd_ref[...].astype(F32)
+    panel_norm = lax.dot_general(
+        jnp.ones((8, 256), F32), panel * panel, (((1,), (1,)), ((), ())),
+        precision=HIGHEST, preferred_element_type=F32,
+    )
+
+    def weights(rows):
+        norm = jnp.sum(rows * rows, axis=-1, keepdims=True)
+        cross = lax.dot_general(
+            rows.astype(BF16), pd_ref[...], (((1,), (1,)), ((), ())), preferred_element_type=F32
+        )
+        scaled = (2.0 / 256.0) * (norm + panel_norm[0:1] - 2.0 * cross)
+        weight = 2.0 * scaled * jnp.exp(-scaled) * (1.0 / math.sqrt(8388608))
+        return lax.dot_general(
+            weight, b_ref[...], (((1,), (1,)), ((), ())),
+            precision=HIGHEST, preferred_element_type=F32,
+        )
+
+    group_slot = {}
+    for g, kind in enumerate(KINDS):
+        group_slot[g] = KINDS[:g].count(kind)
+    pan[...] = jnp.zeros((8, 256), F32)
+    for g, kind in enumerate(KINDS):
+        slot = group_slot[g]
+        rows = []
+        if kind == "A":
+            for zz in range(NZ):
+                for t in range(g * PER, g * PER + PER):
+                    first = pl.multiple_of(zz * 32 + (y // 2) * 16, 16)
+                    pair = u_row[t // 4, t % 4, pl.ds(first, 16), :].astype(F32)
+                    rows.append(jnp.where(y % 2 == 0, pair[0:8], pair[8:16]))
+            near, mine = near_a, z
+        else:
+            wide = [
+                u_row[t // 4, t % 4, pl.ds(pl.multiple_of(z * 32, 32), 32), :].astype(F32)
+                for t in range(g * PER, g * PER + PER)
+            ]
+            for yy in range(NY):
+                for w in wide:
+                    rows.append(w[yy * 8 : yy * 8 + 8])
+            near, mine = near_b, y
+        near[slot] = weights(jnp.concatenate(rows, axis=0))
+        own_c = c_ref[g * 16 : g * 16 + 16, :].astype(F32)
+        own_w = near[slot, pl.ds(pl.multiple_of(mine * 16, 16), 16), :]
+        pan[...] += jnp.sum((own_c * own_w).reshape(2, 8, 256), axis=0)
+    mt[...] = lax.dot_general(
+        f_own[...], c_ref[...], (((0,), (0,)), ((), ())), preferred_element_type=F32
+    )
+
     sibling = (2 * x + 1 - core, c)
-
-    def ucol_forward():
-        return pltpu.make_async_remote_copy(
-            src_ref=u_col, dst_ref=u_col,
-            send_sem=ucol_send.at[0], recv_sem=ucol_recv,
-            device_id=sibling, device_id_type=MESH,
-        )
-
-    pltpu.make_async_copy(u_col, u_col, ucol_recv).wait()
-
-    @pl.when(feeds)
-    def _():
-        ucol_forward().start()
 
     pltpu.make_async_copy(f_buf.at[0], f_buf.at[0], f_recv.at[0]).wait()
     f_swap = pltpu.make_async_remote_copy(
@@ -171,33 +241,6 @@
         device_id=sibling, device_id_type=MESH,
     )
     f_swap.start()
-
-    for u in range(TC):
-        cols = u_col[u].astype(F32)
-        norm = lax.dot_general(
-            jnp.ones((8, 256), F32), cols * cols, (((1,), (1,)), ((), ())),
-            precision=HIGHEST, preferred_element_type=F32,
-        )
-        norm_col[u] = norm * (2.0 * LOG2E / 256.0)
-
-    panel = pd_ref[...].astype(F32)
-    panel_norm = lax.dot_general(
-        jnp.ones((8, 256), F32), panel * panel, (((1,), (1,)), ((), ())),
-        precision=HIGHEST, preferred_element_type=F32,
-    )
-    first_row = pl.multiple_of((c // 2) * 16, 16)
-    own = []
-    for t in range(TR):
-        pair = u_row[t // 4, t % 4, pl.ds(first_row, 16), :].astype(F32)
-        own.append(jnp.where(c % 2 == 0, pair[0:8], pair[8:16]))
-    own = jnp.concatenate(own, axis=0)
-    own_norm = jnp.sum(own * own, axis=-1, keepdims=True)
-    cross = lax.dot_general(
-        own.astype(BF16), pd_ref[...], (((1,), (1,)), ((), ())), preferred_element_type=F32
-    )
-    scaled = (2.0 / 256.0) * (own_norm + panel_norm[0:1] - 2.0 * cross)
-    near[...] = 2.0 * scaled * jnp.exp(-scaled) * (1.0 / math.sqrt(8388608))
-
     f_swap.wait_recv()
 
     @pl.loop(0, 16)
@@ -216,10 +259,6 @@
     here = {"y": y, "z": z}
     lanes = (pl.ds(0, 128), pl.ds(128, 128))
     full = pl.ds(0, 256)
-    group_slot = {}
-    for g, kind in enumerate(KINDS):
-        group_slot[g] = KINDS[:g].count(kind)
-
     def part(g, axis, dest, lane):
         rows = pl.ds(g * PER, PER)
         if KINDS[g] == "A":
@@ -275,6 +314,28 @@
             for u in range(1, TC):
                 out += jnp.dot(s_rel[t, u], f_col[u], preferred_element_type=F32)
             prod[t] = out.reshape(NZ, NY, 8, 256)
+
+    def gather_moment(g):
+        slot = group_slot[g]
+        if KINDS[g] == "A":
+            pieces = [prod[t, zz, y] for zz in range(NZ) for t in range(g * PER, g * PER + PER)]
+            factor = f_z[:, slot * 16 : slot * 16 + 16, :].reshape(NZ * 16, 256)
+            weight = near_a[slot]
+        else:
+            pieces = [prod[t, z, yy] for yy in range(NY) for t in range(g * PER, g * PER + PER)]
+            factor = f_y[:, slot * 16 : slot * 16 + 16, :].reshape(NY * 16, 256)
+            weight = near_b[slot]
+        rows = jnp.concatenate(pieces, axis=0) * (-2.0)
+        pan[...] += jnp.sum((rows * weight).reshape(-1, 8, 256), axis=0)
+        flipped = jnp.transpose(factor.astype(F32)).astype(BF16)
+        high = rows.astype(BF16)
+        rest = rows - high.astype(F32)
+        middle = rest.astype(BF16)
+        low = (rest - middle.astype(F32)).astype(BF16)
+        out = jnp.dot(flipped, low, preferred_element_type=F32)
+        out += jnp.dot(flipped, middle, preferred_element_type=F32)
+        out += jnp.dot(flipped, high, preferred_element_type=F32)
+        mt[...] += out
 
     def step(g, k):
         axes = ("y", "z") if KINDS[g] == "A" else ("z", "y")
@@ -296,55 +357,71 @@
         if k == first:
             for way in range(2):
                 copy_of(g, axes[1], 0, way).start()
-
-    def slope_unit(n, acc):
-        t, u = n // TC, n % TC
-        cross = lax.dot_general(
-            u_row[t // 4, t % 4], u_col[u], (((1,), (1,)), ((), ())), preferred_element_type=F32
-        )
-        across = norm_col[u]
-        for k in range(0, 256, 32):
-            down = norm_row[t, k : k + 32]
-            norms = jnp.concatenate([down, down], axis=1) + across[0:1]
-            minus = cross[k : k + 32] * (4.0 * LOG2E / 256.0) - norms
-            term = s_rel[t, u, k : k + 32].astype(F32) * (minus * jnp.exp2(minus))
-            acc = acc + jnp.sum(term.reshape(4, 8, 256), axis=0)
+            gather_moment(g)
+
+    def slope_row(t, acc):
+        for u in range(TC):
+            cross = lax.dot_general(
+                u_row[t // 4, t % 4], u_col[u], (((1,), (1,)), ((), ())), preferred_element_type=F32
+            )
+            across = norm_col[u]
+            for k in range(0, 256, 32):
+                down = norm_row[t, k : k + 32]
+                norms = jnp.concatenate([down, down], axis=1) + across[0:1]
+                minus = cross[k : k + 32] * (4.0 * LOG2E / 256.0) - norms
+                term = s_rel[t, u, k : k + 32].astype(F32) * (minus * jnp.exp2(minus))
+                acc = acc + jnp.sum(term.reshape(4, 8, 256), axis=0)
         return acc
 
+    def ucol_forward():
+        return pltpu.make_async_remote_copy(
+            src_ref=u_col, dst_ref=u_col,
+            send_sem=ucol_send.at[0], recv_sem=ucol_recv,
+            device_id=sibling, device_id_type=MESH,
+        )
+
     n_groups = len(KINDS)
-    n_units = TR * TC
+    for g in range(n_groups):
+        step(g, 0)
+
+    pltpu.make_async_copy(u_col, u_col, ucol_recv).wait()
+
+    @pl.when(feeds)
+    def _():
+        ucol_forward().start()
+
+    for u in range(TC):
+        cols = u_col[u].astype(F32)
+        norm = lax.dot_general(
+            jnp.ones((8, 256), F32), cols * cols, (((1,), (1,)), ((), ())),
+            precision=HIGHEST, preferred_element_type=F32,
+        )
+        norm_col[u] = norm * (2.0 * LOG2E / 256.0)
+
+    for d in range(1, NZ):
+        fz_to(d).wait_recv()
+    for d in range(1, NY):
+        fy_to(d).wait_recv()
+
     acc = jnp.zeros((8, 256), F32)
     done = 0
-    for g in range(n_groups):
-        step(g, 0)
-    visits = (STEPS - 1) * n_groups
-    busy = visits - 4
-    for visit in range(visits):
-        until = min(n_units, n_units * (visit + 1) // busy)
-        if until > done:
-            acc = lax.fori_loop(done, until, slope_unit, acc)
-            done = until
-        step(visit % n_groups, 1 + visit // n_groups)
+    for k in range(1, 5):
+        if k < 3:
+            for half in range(2):
+                acc = lax.fori_loop(done, done + 4, slope_row, acc)
+                done += 4
+                for g in range(half * n_groups // 2, (half + 1) * n_groups // 2):
+                    step(g, k)
+        else:
+            for g in range(n_groups):
+                step(g, k)
     trail = jnp.sum(acc) * (-2.0 / LOG2E / 32768.0)
-
-    for t in range(TR):
-        total[pl.ds(t * 8, 8), :] = (
-            c_ref[pl.ds((t // 2) * 16, 16), :].astype(F32)[(t % 2) * 8 : (t % 2) * 8 + 8]
-            - 2.0 * prod[t, z, y]
-        )
-    whole = total[...]
-    adjoint = jnp.dot(whole, b_ref[...], precision=HIGHEST, preferred_element_type=F32)
-    adj_ref[...] = adjoint
-    moment = lax.dot_general(
-        whole, f_own[...].astype(F32), (((0,), (0,)), ((), ())),
-        precision=HIGHEST, preferred_element_type=F32,
-    )
-    panel_part = jnp.sum(adjoint * near[...])
+    panel_part = jnp.sum(pan[...])
     lane = lax.broadcasted_iota(jnp.int32, (8, 256), 1)
     down = lax.broadcasted_iota(jnp.int32, (8, 256), 0)
     for p in range(NR * NY):
-        block = jnp.where(jnp.logical_and(down == 0, lane == 254), trail, moment[8 * p : 8 * p + 8])
-        m1[p] = jnp.where(jnp.logical_and(down == 0, lane == 255), panel_part, block)
+        block = jnp.where(jnp.logical_and(down == 7, lane == 0), trail, mt[8 * p : 8 * p + 8])
+        m1[p] = jnp.where(jnp.logical_and(down == 7, lane == 1), panel_part, block)
 
     def exchange(base, n, me, dev, src, dst):
         def copy(d):
@@ -355,34 +432,50 @@
                 device_id=dev(peer), device_id_type=MESH,
             )
 
-        @pl.loop(1, n)
-        def _(d):
-            copy(d).start()
-
-        @pl.loop(1, n)
-        def _(d):
-            copy(d).wait()
-
+        def start():
+            @pl.loop(1, n)
+            def _(d):
+                copy(d).start()
+
+        def wait():
+            @pl.loop(1, n)
+            def _(d):
+                copy(d).wait()
+
+        return start, wait
+
+    start, wait = exchange(0, NR * NY, place, near_dev, lambda p: m1.at[p], m1r)
     m1r[place] = m1[place]
-    exchange(0, NR * NY, place, near_dev, lambda p: m1.at[p], m1r)
+    start()
+    for g in range(n_groups):
+        step(g, 5)
+    wait()
     part1 = m1r[0]
     for j in range(1, NR * NY):
         part1 = part1 + m1r[j]
     m3[z] = part1
-    exchange(32, NZ, z, lambda p: (r, p * NY + y), lambda p: m3.at[z], m3)
+    start, wait = exchange(32, NZ, z, lambda p: (r, p * NY + y), lambda p: m3.at[z], m3)
+    start()
+    for g in range(n_groups):
+        step(g, 6)
+
+    for t in range(TR):
+        total[pl.ds(t * 8, 8), :] = (
+            c_ref[pl.ds((t // 2) * 16, 16), :].astype(F32)[(t % 2) * 8 : (t % 2) * 8 + 8]
+            - 2.0 * prod[t, z, y]
+        )
+    adj_ref[...] = jnp.dot(total[...], b_ref[...], precision=HIGHEST, preferred_element_type=F32)
+
+    wait()
     part3 = m3[0]
     for j in range(1, NZ):
         part3 = part3 + m3[j]
     m5[place] = part3
-    exchange(40, NR * NY, place, near_dev, lambda p: m5.at[place], m5)
-    diag = lax.dot_general(
-        b_ref[...], m5[...].reshape(256, 256), (((0,), (0,)), ((), ())),
-        precision=HIGHEST, preferred_element_type=F32,
-    )
-    down = lax.broadcasted_iota(jnp.int32, (256, 256), 0)
-    across = lax.broadcasted_iota(jnp.int32, (256, 256), 1)
-    diag_ref[...] = jnp.where(down >= across, -diag, 0.0)
-    slope_ref[...] = part3[0:1, 254:256]
+    start, wait = exchange(40, NR * NY, place, near_dev, lambda p: m5.at[place], m5)
+    start()
+    slope_ref[...] = part3[7:8, 0:2]
+    wait()
+    moment_ref[...] = m5[...]
 
     @pl.loop(0, 16)
     def _(n):
@@ -404,11 +497,27 @@
         ucol_forward().wait_send()
 
     f_swap.wait_send()
+    for d in range(1, NZ):
+        fz_to(d).wait_send()
+    for d in range(1, NY):
+        fy_to(d).wait_send()
     for g, kind in enumerate(KINDS):
         for axis in "yz":
             for rnd in range(size[axis] // 2):
                 for way in range(2):
                     copy_of(g, axis, rnd, way).wait_send()
+
+
+def finish(adj_in, m_in, slope_in, b_ref, adj_ref, diag_ref, slope_ref):
+    adj_ref[...] = adj_in[...]
+    slope_ref[...] = slope_in[...]
+    diag = lax.dot_general(
+        b_ref[...], m_in[...], (((0,), (1,)), ((), ())),
+        precision=HIGHEST, preferred_element_type=F32,
+    )
+    down = lax.broadcasted_iota(jnp.int32, (256, 256), 0)
+    across = lax.broadcasted_iota(jnp.int32, (256, 256), 1)
+    diag_ref[...] = jnp.where(down >= across, -diag, 0.0)
 
 
 def local(trailing_cot, panel_factor, panel_cot, block_inverse, row_desc, panel_desc):
@@ -417,11 +526,11 @@
     vmem = pl.BlockSpec(memory_space=pltpu.VMEM)
     dma = pltpu.SemaphoreType.DMA
     V = pltpu.VMEM
-    adjoint, diag, slope = pl.pallas_call(
+    adjoint, moment, slope = pl.pallas_call(
         kernel,
         out_shape=(
             jax.ShapeDtypeStruct((128, 256), F32),
-            jax.ShapeDtypeStruct((256, 256), F32),
+            jax.ShapeDtypeStruct((NR * NY, 8, 256), F32),
             jax.ShapeDtypeStruct((1, 2), F32),
         ),
         in_specs=[hbm, hbm, vmem, vmem, vmem, vmem],
@@ -437,9 +546,14 @@
             V((4, 32, 256), BF16),
             V((2, 16, 32, 256), BF16),
             V((TC, 256, 256), BF16),
+            V((NZ, N_A * 16, 256), BF16),
+            V((NY, N_B * 16, 256), BF16),
             V((TR, NZ, NY, 8, 256), F32),
             V((128, 256), F32),
-            V((128, 256), F32),
+            V((N_A, NZ * 16, 256), F32),
+            V((N_B, NY * 16, 256), F32),
+            V((256, 256), F32),
+            V((8, 256), F32),
             V((N_A, 2, PER, NZ, 8, 128), F32),
             V((N_A, 2, 1, PER, NZ, 8, 256), F32),
             V((N_A, 2, PER, 8, 128), F32),
@@ -457,6 +571,8 @@
             dma((16,)),
             dma((2,)),
             dma,
+            dma((NZ + NY,)),
+            dma((NZ + NY,)),
             dma((4,)),
             dma,
             dma((len(KINDS) * 12,)),
@@ -479,6 +595,17 @@
         block_inverse,
         panel_desc,
     )
+    adjoint, diag, slope = pl.pallas_call(
+        finish,
+        out_shape=(
+            jax.ShapeDtypeStruct((128, 256), F32),
+            jax.ShapeDtypeStruct((256, 256), F32),
+            jax.ShapeDtypeStruct((1, 2), F32),
+        ),
+        in_specs=[vmem] * 4,
+        out_specs=(vmem, vmem, vmem),
+        name="finish",
+    )(adjoint, moment.reshape(256, 256), slope, block_inverse)
     return adjoint.reshape(16, 8, 256), diag, slope.reshape(2)
 
 

time: 98.6 us -> 87.1 us (0.88)
  Pallas kernels: 93.5 us -> 86.3 us
  local copies, waits for them, and re-layouts: 4.35 us -> 0 us
    pallas_call x1, Pallas kernels: 93.5 us -> 84.1 us  [local(): pl.pallas_call(kernel, out_shape=(jax.ShapeDtypeStruct((128, 256), F32),...]
    unnamed x3 -> x0, local copies, waits for them, and re-layouts: 4.35 us -> none
    pallas_call x0 -> x1, Pallas kernels: none -> 2.23 us  [local(): pl.pallas_call(finish, out_shape=(jax.ShapeDtypeStruct((128, 256), F32),...]
where the time goes in v3:
time: 87.1 us; the launch traced here: 87 us
  Pallas kernels  86.3 us (99%)
    pallas_call x1, Pallas kernels, local(): pl.pallas_call(kernel, out_shape=(jax.ShapeDtypeStruct((128, 256), F32),...  84.1 us
    pallas_call x1, Pallas kernels, local(): pl.pallas_call(finish, out_shape=(jax.ShapeDtypeStruct((128, 256), F32),...  2.23 us

profile of v3, /device:TPU:1, one launch (start us, length us, event | category | flops | bytes accessed | tf_op | source)
XLA Modules:
  0.0 87.0 jit_solution(14074144038414500927)
XLA Ops:
  0.6 84.1 %panel_step.1 = (f32[128,256]{1,0:T(8,128)}, f32[32,8,256]{2,1,0:T(8,128)}, f32[1,2]{1,0:T(1,128)}) custom-call(bf16[4,4,256,256]{3,2,1,0:T(8,128)(2,1)} %bitcast.13, bf16[32768,128]{1,0:T(8,128)(2,1)} %bitcast.12, bf16[128,256]{1,0:T(8,128)(2,1)} %bitcast.15, bf16[128,256]{1,0:T(8,128)(2,1)} %bitcast.16, f32[256,256]{1,0:T(8,128)} %b_ref.3, ...), custom_call_target="tpu_custom_call" | custom-call | flops 4294967296 | bytes 12582912 | tf_op jit(solution)/shard_map/panel_step/pallas_call | solution.py:529
  84.7 2.2 %finish.1 = (f32[128,256]{1,0:T(8,128)}, f32[256,256]{1,0:T(8,128)}, f32[1,2]{1,0:T(1,128)}) custom-call(f32[128,256]{1,0:T(8,128)} %get-tuple-element.9.adj_in, f32[256,256]{1,0:T(8,128)} %bitcast.11, f32[1,2]{1,0:T(1,128)} %get-tuple-element.11.slope_in, f32[256,256]{1,0:T(8,128)} %b_ref.3), custom_call_target="tpu_custom_call" | custom-call | tf_op jit(solution)/shard_map/finish/pallas_call | solution.py:598

commit v4 on v3

--- a/solution.py
+++ b/solution.py
@@ -25,13 +25,32 @@
 STEPS = 7
 
 
+SCHEDULE = [
+    ("send",), ("step", 7, 0), ("step", 3, 0), ("step", 5, 0), ("step", 1, 0), ("step", 6, 0), ("step", 7, 1),
+    ("step", 2, 0), ("step", 3, 1), ("pass", 1), ("step", 4, 0), ("step", 5, 1), ("step", 1, 1),
+    ("step", 0, 0), ("ucol",), ("slope", 1), ("step", 6, 1), ("step", 7, 2), ("slope", 1), ("pass", 2),
+    ("slope", 1), ("step", 2, 1), ("step", 3, 2), ("slope", 1), ("slope", 1), ("step", 4, 1), ("step", 5, 2),
+    ("slope", 1), ("pass", 3), ("slope", 1), ("step", 0, 1), ("step", 1, 2), ("slope", 1), ("slope", 1),
+    ("step", 7, 3), ("slope", 1), ("slope", 1), ("step", 6, 2), ("step", 3, 3), ("factors",), ("moment", 6),
+    ("slope", 1), ("slope", 1), ("step", 5, 3), ("slope", 1), ("slope", 1), ("step", 2, 2), ("step", 1, 3),
+    ("moment", 2), ("slope", 1), ("step", 7, 4), ("step", 6, 3), ("moment", 7), ("step", 4, 2), ("moment", 4),
+    ("step", 3, 4), ("moment", 3), ("step", 5, 4), ("step", 2, 3), ("moment", 5), ("step", 0, 2),
+    ("step", 7, 5), ("moment", 0), ("step", 1, 4), ("step", 6, 4), ("step", 4, 3), ("step", 3, 5),
+    ("moment", 1), ("sum1",), ("step", 2, 4), ("step", 0, 3), ("step", 5, 5), ("step", 7, 6), ("step", 1, 5),
+    ("step", 6, 5), ("step", 4, 4), ("step", 3, 6), ("step", 2, 5), ("step", 0, 4), ("sum2",), ("step", 5, 6),
+    ("step", 1, 6), ("step", 6, 6), ("step", 4, 5), ("step", 2, 6), ("step", 0, 5), ("step", 4, 6),
+    ("step", 0, 6),
+]
+
+
 def kernel(
-    u_hbm, s_hbm, c_ref, f_own, b_ref, pd_ref,
-    adj_ref, moment_ref, slope_ref,
-    s_raw, s_f32, s_rel, u_row, u_col, norm_row, norm_col, f_parts, f_buf, f_col, f_z, f_y, prod, total, near_a, near_b, mt, pan,
+    u_hbm, s_hbm, c_hbm, f_hbm, b_hbm, pd_hbm,
+    adj_hbm, moment_ref, slope_ref,
+    c_ref, f_own, b_ref, pd_ref, adj_ref,
+    s_raw, s_f32, s_rel, u_row, u_col, norm_row, norm_col, f_parts, f_buf, f_col, f_z, f_y, prod, total, near_a, near_b, q_a, q_b, mt, pan,
     ay1, ay2, az1, az2, bz1, bz2, by1, by2,
     m1, m1r, m3, m5,
-    s_sem, u_sem, f_send, f_recv, f_local, fz_send, fz_recv, ucol_send, ucol_recv, rs_send, rs_recv, m_send, m_recv,
+    s_sem, in_sem, u_sem, f_send, f_recv, f_local, fz_send, fz_recv, ucol_send, ucol_recv, rs_send, rs_recv, m_send, m_recv,
 ):
     r = lax.axis_index("row")
     c = lax.axis_index("col")
@@ -79,12 +98,22 @@
         for t in range(TR)
     ]
     u_copy = pltpu.make_async_copy(u_hbm, u_row, u_sem)
+    f_copy = pltpu.make_async_copy(f_hbm, f_own, in_sem.at[0])
+    small = [
+        pltpu.make_async_copy(c_hbm, c_ref, in_sem.at[1]),
+        pltpu.make_async_copy(b_hbm, b_ref, in_sem.at[2]),
+        pltpu.make_async_copy(pd_hbm, pd_ref, in_sem.at[3]),
+    ]
+    f_copy.start()
     for cp in s_copies[:2]:
         cp.start()
     u_copy.start()
+    for cp in small:
+        cp.start()
     for cp in s_copies[2:]:
         cp.start()
 
+    f_copy.wait()
     f_wide = f_own[...].astype(F32)
     for q in range(4):
         f_parts[q] = jnp.concatenate(
@@ -146,11 +175,13 @@
     def _():
         pltpu.make_async_copy(u_hbm.at[:, quarter], u_col, ucol_recv).start()
 
-    def fz_to(d):
+    def fz_to(rnd, way):
+        sign = 1 if way == 0 else NZ - 1
+        held = (z + (NZ - sign) * rnd) % NZ
         return pltpu.make_async_remote_copy(
-            src_ref=f_z.at[z], dst_ref=f_z.at[z],
-            send_sem=fz_send.at[d], recv_sem=fz_recv.at[d],
-            device_id=(r, ((z + d) % NZ) * NY + y), device_id_type=MESH,
+            src_ref=f_z.at[held], dst_ref=f_z.at[held],
+            send_sem=fz_send.at[4 * way + rnd], recv_sem=fz_recv.at[4 * way + rnd],
+            device_id=(r, ((z + sign) % NZ) * NY + y), device_id_type=MESH,
         )
 
     def fy_to(d):
@@ -160,14 +191,6 @@
             device_id=(r, z * NY + (y + d) % NY), device_id_type=MESH,
         )
 
-    @pl.loop(1, NZ)
-    def _(d):
-        fz_to(d).start()
-
-    @pl.loop(1, NY)
-    def _(d):
-        fy_to(d).start()
-
     for t in range(EARLY, TR):
         s_copies[t].wait()
 
@@ -176,6 +199,8 @@
         relay(t)
 
     u_copy.wait()
+    for cp in small:
+        cp.wait()
 
     @pl.loop(0, TR)
     def _(t):
@@ -241,9 +266,10 @@
         device_id=sibling, device_id_type=MESH,
     )
     f_swap.start()
+
     f_swap.wait_recv()
 
-    @pl.loop(0, 16)
+    @pl.loop(0, 16, unroll=4)
     def _(m):
         even = f_buf[0, m].astype(F32)
         odd = f_buf[1, m].astype(F32)
@@ -315,17 +341,26 @@
                 out += jnp.dot(s_rel[t, u], f_col[u], preferred_element_type=F32)
             prod[t] = out.reshape(NZ, NY, 8, 256)
 
+    def keep_rows(g):
+        slot = group_slot[g]
+        span = range(g * PER, g * PER + PER)
+        if KINDS[g] == "A":
+            for n, piece in enumerate(prod[t, zz, y] for zz in range(NZ) for t in span):
+                q_a[slot, n] = piece * (-2.0)
+        else:
+            for n, piece in enumerate(prod[t, z, yy] for yy in range(NY) for t in span):
+                q_b[slot, n] = piece * (-2.0)
+
     def gather_moment(g):
         slot = group_slot[g]
         if KINDS[g] == "A":
-            pieces = [prod[t, zz, y] for zz in range(NZ) for t in range(g * PER, g * PER + PER)]
+            rows = q_a[slot].reshape(NZ * 16, 256)
             factor = f_z[:, slot * 16 : slot * 16 + 16, :].reshape(NZ * 16, 256)
             weight = near_a[slot]
         else:
-            pieces = [prod[t, z, yy] for yy in range(NY) for t in range(g * PER, g * PER + PER)]
+            rows = q_b[slot].reshape(NY * 16, 256)
             factor = f_y[:, slot * 16 : slot * 16 + 16, :].reshape(NY * 16, 256)
             weight = near_b[slot]
-        rows = jnp.concatenate(pieces, axis=0) * (-2.0)
         pan[...] += jnp.sum((rows * weight).reshape(-1, 8, 256), axis=0)
         flipped = jnp.transpose(factor.astype(F32)).astype(BF16)
         high = rows.astype(BF16)
@@ -357,7 +392,7 @@
         if k == first:
             for way in range(2):
                 copy_of(g, axes[1], 0, way).start()
-            gather_moment(g)
+            keep_rows(g)
 
     def slope_row(t, acc):
         for u in range(TC):
@@ -381,83 +416,131 @@
         )
 
     n_groups = len(KINDS)
-    for g in range(n_groups):
-        step(g, 0)
-
-    pltpu.make_async_copy(u_col, u_col, ucol_recv).wait()
-
-    @pl.when(feeds)
-    def _():
-        ucol_forward().start()
-
-    for u in range(TC):
-        cols = u_col[u].astype(F32)
-        norm = lax.dot_general(
-            jnp.ones((8, 256), F32), cols * cols, (((1,), (1,)), ((), ())),
-            precision=HIGHEST, preferred_element_type=F32,
-        )
-        norm_col[u] = norm * (2.0 * LOG2E / 256.0)
-
-    for d in range(1, NZ):
-        fz_to(d).wait_recv()
-    for d in range(1, NY):
-        fy_to(d).wait_recv()
+
+    def take_ucol():
+        pltpu.make_async_copy(u_col, u_col, ucol_recv).wait()
+
+        @pl.when(feeds)
+        def _():
+            ucol_forward().start()
+
+        for u in range(TC):
+            cols = u_col[u].astype(F32)
+            norm = lax.dot_general(
+                jnp.ones((8, 256), F32), cols * cols, (((1,), (1,)), ((), ())),
+                precision=HIGHEST, preferred_element_type=F32,
+            )
+            norm_col[u] = norm * (2.0 * LOG2E / 256.0)
+
+    def send_factors():
+        for way in range(2):
+            fz_to(0, way).start()
+
+        @pl.loop(1, NY)
+        def _(d):
+            fy_to(d).start()
+
+    def pass_factors(rnd):
+        for way in range(2):
+            fz_to(rnd - 1, way).wait_recv()
+            if rnd + way < 4:
+                fz_to(rnd, way).start()
+
+    def take_factors():
+        fz_to(3, 0).wait_recv()
+        for d in range(1, NY):
+            fy_to(d).wait_recv()
+
+    near = []
+    for dx in range(NX):
+        for dk in range(2):
+            for dy in range(NY):
+                if dx or dk or dy:
+                    near.append((min(dx, NX - dx) + min(dy, NY - dy) + 0.1 * dk, dx, dk, dy))
+    near.sort(reverse=True)
+    xs = [((x + d) % NX) * 2 for d in range(NX)]
+    ks = [core, 1 - core]
+    ys = [(y + d) % NY for d in range(NY)]
+
+    def to_near(stage, src, dst):
+        out = []
+        for _, dx, dk, dy in near:
+            row = xs[dx] + ks[dk]
+            out.append(pltpu.make_async_remote_copy(
+                src_ref=src(row * NY + ys[dy]), dst_ref=dst,
+                send_sem=m_send.at[stage], recv_sem=m_recv.at[stage],
+                device_id=(row, z * NY + ys[dy]), device_id_type=MESH,
+            ))
+        return out
+
+    copies1 = to_near(0, lambda p: m1.at[p], m1r.at[place])
+    copies3 = to_near(2, lambda p: m5.at[place], m5.at[place])
+    copies2 = [
+        pltpu.make_async_remote_copy(
+            src_ref=m3.at[z], dst_ref=m3.at[z],
+            send_sem=m_send.at[1], recv_sem=m_recv.at[1],
+            device_id=(r, ((z + d) % NZ) * NY + y), device_id_type=MESH,
+        )
+        for d in (4, 3, 5, 2, 6, 1, 7)
+    ]
+
+    def wait_all(ref, n, sem):
+        blocks = ref.at[pl.ds(0, n)]
+        pltpu.make_async_copy(blocks, blocks, sem).wait()
+
+    def sum_first(acc):
+        trail = jnp.sum(acc) * (-2.0 / LOG2E / 32768.0)
+        panel_part = jnp.sum(pan[...])
+        lane = lax.broadcasted_iota(jnp.int32, (8, 256), 1)
+        down = lax.broadcasted_iota(jnp.int32, (8, 256), 0)
+        for p in range(NR * NY):
+            block = jnp.where(jnp.logical_and(down == 7, lane == 0), trail, mt[8 * p : 8 * p + 8])
+            m1[p] = jnp.where(jnp.logical_and(down == 7, lane == 1), panel_part, block)
+        m1r[place] = m1[place]
+        for cp in copies1:
+            cp.start()
+
+    def sum_second():
+        wait_all(m1r, NR * NY - 1, m_recv.at[0])
+        part = m1r[0]
+        for j in range(1, NR * NY):
+            part = part + m1r[j]
+        m3[z] = part
+        for cp in copies2:
+            cp.start()
+
+    def sum_third():
+        wait_all(m3, NZ - 1, m_recv.at[1])
+        part = m3[0]
+        for j in range(1, NZ):
+            part = part + m3[j]
+        m5[place] = part
+        for cp in copies3:
+            cp.start()
+        slope_ref[...] = part[7:8, 0:2]
 
     acc = jnp.zeros((8, 256), F32)
     done = 0
-    for k in range(1, 5):
-        if k < 3:
-            for half in range(2):
-                acc = lax.fori_loop(done, done + 4, slope_row, acc)
-                done += 4
-                for g in range(half * n_groups // 2, (half + 1) * n_groups // 2):
-                    step(g, k)
-        else:
-            for g in range(n_groups):
-                step(g, k)
-    trail = jnp.sum(acc) * (-2.0 / LOG2E / 32768.0)
-    panel_part = jnp.sum(pan[...])
-    lane = lax.broadcasted_iota(jnp.int32, (8, 256), 1)
-    down = lax.broadcasted_iota(jnp.int32, (8, 256), 0)
-    for p in range(NR * NY):
-        block = jnp.where(jnp.logical_and(down == 7, lane == 0), trail, mt[8 * p : 8 * p + 8])
-        m1[p] = jnp.where(jnp.logical_and(down == 7, lane == 1), panel_part, block)
-
-    def exchange(base, n, me, dev, src, dst):
-        def copy(d):
-            peer = (me + d) % n
-            return pltpu.make_async_remote_copy(
-                src_ref=src(peer), dst_ref=dst.at[me],
-                send_sem=m_send.at[base + d], recv_sem=m_recv.at[base + d],
-                device_id=dev(peer), device_id_type=MESH,
-            )
-
-        def start():
-            @pl.loop(1, n)
-            def _(d):
-                copy(d).start()
-
-        def wait():
-            @pl.loop(1, n)
-            def _(d):
-                copy(d).wait()
-
-        return start, wait
-
-    start, wait = exchange(0, NR * NY, place, near_dev, lambda p: m1.at[p], m1r)
-    m1r[place] = m1[place]
-    start()
-    for g in range(n_groups):
-        step(g, 5)
-    wait()
-    part1 = m1r[0]
-    for j in range(1, NR * NY):
-        part1 = part1 + m1r[j]
-    m3[z] = part1
-    start, wait = exchange(32, NZ, z, lambda p: (r, p * NY + y), lambda p: m3.at[z], m3)
-    start()
-    for g in range(n_groups):
-        step(g, 6)
+    for event in SCHEDULE:
+        if event[0] == "step":
+            step(event[1], event[2])
+        elif event[0] == "slope":
+            acc = lax.fori_loop(done, done + event[1], slope_row, acc)
+            done += event[1]
+        elif event[0] == "ucol":
+            take_ucol()
+        elif event[0] == "send":
+            send_factors()
+        elif event[0] == "pass":
+            pass_factors(event[1])
+        elif event[0] == "moment":
+            gather_moment(event[1])
+        elif event[0] == "factors":
+            take_factors()
+        elif event[0] == "sum1":
+            sum_first(acc)
+        elif event[0] == "sum2":
+            sum_second()
 
     for t in range(TR):
         total[pl.ds(t * 8, 8), :] = (
@@ -465,18 +548,17 @@
             - 2.0 * prod[t, z, y]
         )
     adj_ref[...] = jnp.dot(total[...], b_ref[...], precision=HIGHEST, preferred_element_type=F32)
-
-    wait()
-    part3 = m3[0]
-    for j in range(1, NZ):
-        part3 = part3 + m3[j]
-    m5[place] = part3
-    start, wait = exchange(40, NR * NY, place, near_dev, lambda p: m5.at[place], m5)
-    start()
-    slope_ref[...] = part3[7:8, 0:2]
-    wait()
+    adj_copy = pltpu.make_async_copy(adj_ref, adj_hbm, in_sem.at[4])
+    adj_copy.start()
+
+    sum_third()
+    wait_all(m5, NR * NY - 1, m_recv.at[2])
     moment_ref[...] = m5[...]
 
+    adj_copy.wait()
+    wait_all(m1r, NR * NY - 1, m_send.at[0])
+    wait_all(m3, NZ - 1, m_send.at[1])
+    wait_all(m5, NR * NY - 1, m_send.at[2])
     @pl.loop(0, 16)
     def _(n):
         q, xd = n // NX, n % NX
@@ -497,8 +579,10 @@
         ucol_forward().wait_send()
 
     f_swap.wait_send()
-    for d in range(1, NZ):
-        fz_to(d).wait_send()
+    for rnd in range(4):
+        for way in range(2):
+            if rnd + way < 4:
+                fz_to(rnd, way).wait_send()
     for d in range(1, NY):
         fy_to(d).wait_send()
     for g, kind in enumerate(KINDS):
@@ -533,9 +617,14 @@
             jax.ShapeDtypeStruct((NR * NY, 8, 256), F32),
             jax.ShapeDtypeStruct((1, 2), F32),
         ),
-        in_specs=[hbm, hbm, vmem, vmem, vmem, vmem],
-        out_specs=(vmem, vmem, vmem),
+        in_specs=[hbm] * 6,
+        out_specs=(hbm, vmem, vmem),
         scratch_shapes=[
+            V((128, 256), BF16),
+            V((128, 256), BF16),
+            V((256, 256), F32),
+            V((256, 256), BF16),
+            V((128, 256), F32),
             V((TR, 2048, 128), BF16),
             V((2048, 128), F32),
             V((TR, TC, 256, 256), BF16),
@@ -552,6 +641,8 @@
             V((128, 256), F32),
             V((N_A, NZ * 16, 256), F32),
             V((N_B, NY * 16, 256), F32),
+            V((N_A, NZ * 2, 8, 256), F32),
+            V((N_B, NY * 2, 8, 256), F32),
             V((256, 256), F32),
             V((8, 256), F32),
             V((N_A, 2, PER, NZ, 8, 128), F32),
@@ -567,6 +658,7 @@
             V((NZ, 8, 256), F32),
             V((NR * NY, 8, 256), F32),
             dma((TR,)),
+            dma((5,)),
             dma,
             dma((16,)),
             dma((2,)),
@@ -577,8 +669,8 @@
             dma,
             dma((len(KINDS) * 12,)),
             dma((len(KINDS) * 12,)),
-            dma((72,)),
-            dma((72,)),
+            dma((3,)),
+            dma((3,)),
         ],
         compiler_params=pltpu.CompilerParams(
             collective_id=0, has_side_effects=True, vmem_limit_bytes=60 * 1024 * 1024

time: 87.1 us -> 77.7 us (0.89)
  Pallas kernels: 86.3 us -> 77 us
    pallas_call x1, Pallas kernels: 84.1 us -> 74.7 us  [local(): pl.pallas_call(kernel, out_shape=(jax.ShapeDtypeStruct((128, 256), F32),...]
where the time goes in v4:
time: 77.7 us; the launch traced here: 77.6 us
  Pallas kernels  77 us (99%)
    pallas_call x1, Pallas kernels, local(): pl.pallas_call(kernel, out_shape=(jax.ShapeDtypeStruct((128, 256), F32),...  74.7 us
    pallas_call x1, Pallas kernels, local(): pl.pallas_call(finish, out_shape=(jax.ShapeDtypeStruct((128, 256), F32),...  2.23 us

profile of v4, /device:TPU:1, one launch (start us, length us, event | category | flops | bytes accessed | tf_op | source)
XLA Modules:
  0.0 77.6 jit_solution(8945486049948113920)
XLA Ops:
  0.6 74.7 %panel_step.1 = (f32[128,256]{1,0:T(8,128)}, f32[32,8,256]{2,1,0:T(8,128)}, f32[1,2]{1,0:T(1,128)}) custom-call(bf16[4,4,256,256]{3,2,1,0:T(8,128)(2,1)} %bitcast.13, bf16[32768,128]{1,0:T(8,128)(2,1)} %bitcast.12, bf16[128,256]{1,0:T(8,128)(2,1)} %bitcast.15, bf16[128,256]{1,0:T(8,128)(2,1)} %bitcast.16, f32[256,256]{1,0:T(8,128)} %b_ref.1, ...), custom_call_target="tpu_custom_call" | custom-call | flops 4294967296 | bytes 12582912 | tf_op jit(solution)/shard_map/panel_step/pallas_call | solution.py:613
  75.4 2.2 %finish.1 = (f32[128,256]{1,0:T(8,128)}, f32[256,256]{1,0:T(8,128)}, f32[1,2]{1,0:T(1,128)}) custom-call(f32[128,256]{1,0:T(8,128)} %get-tuple-element.9.adj_in, f32[256,256]{1,0:T(8,128)} %bitcast.11, f32[1,2]{1,0:T(1,128)} %get-tuple-element.11.slope_in, f32[256,256]{1,0:T(8,128)} %b_ref.1), custom_call_target="tpu_custom_call" | custom-call | tf_op jit(solution)/shard_map/finish/pallas_call | solution.py:690

commit v5 on v4

--- a/solution.py
+++ b/solution.py
@@ -21,13 +21,13 @@
 KINDS = "ABABABAB"
 N_A = KINDS.count("A")
 N_B = KINDS.count("B")
-EARLY = 6
+EARLY = 3
 STEPS = 7
 
 
 SCHEDULE = [
     ("send",), ("step", 7, 0), ("step", 3, 0), ("step", 5, 0), ("step", 1, 0), ("step", 6, 0), ("step", 7, 1),
-    ("step", 2, 0), ("step", 3, 1), ("pass", 1), ("step", 4, 0), ("step", 5, 1), ("step", 1, 1),
+    ("step", 2, 0), ("step", 3, 1), ("pass", 1), ("step", 4, 0), ("upass",), ("step", 5, 1), ("step", 1, 1),
     ("step", 0, 0), ("ucol",), ("slope", 1), ("step", 6, 1), ("step", 7, 2), ("slope", 1), ("pass", 2),
     ("slope", 1), ("step", 2, 1), ("step", 3, 2), ("slope", 1), ("slope", 1), ("step", 4, 1), ("step", 5, 2),
     ("slope", 1), ("pass", 3), ("slope", 1), ("step", 0, 1), ("step", 1, 2), ("slope", 1), ("slope", 1),
@@ -80,18 +80,23 @@
         def _():
             greet((root, 2 * m + core))
 
-    @pl.loop(1, NR * NY)
-    def _(d):
-        greet(near_dev((place + d) % (NR * NY)))
-
-    @pl.loop(1, NZ)
-    def _(d):
-        greet((r, ((z + d) % NZ) * NY + y))
-
     @pl.when(jnp.logical_and(feeds, jnp.logical_not(is_root)))
     def _():
         for u in range(TC):
             greet((root, partner(u)))
+
+    xs = [((x + d) % NX) * 2 for d in range(NX)]
+    ks = [core, 1 - core]
+    ys = [(y + d) % NY for d in range(NY)]
+    for dx in (2, 1, 3, 0):
+        for dy in (2, 1, 3, 0):
+            for dk in range(2):
+                if dx or dk or dy:
+                    greet((xs[dx] + ks[dk], z * NY + ys[dy]))
+
+    @pl.loop(1, NZ)
+    def _(d):
+        greet((r, ((z + d) % NZ) * NY + y))
 
     s_copies = [
         pltpu.make_async_copy(s_hbm.at[pl.ds(t * 2048, 2048)], s_raw.at[t], s_sem.at[t])
@@ -141,9 +146,15 @@
 
     pl.semaphore_wait(barrier, 16 + 31 + 7 - jnp.where(is_root, 1, 0) + jnp.where(feeds, 3, 0))
 
+    def far_first(n):
+        dq, dx = n // NX, n % NX
+        dq = jnp.where(dq < 2, 2 - dq, 3 * (3 - dq))
+        dx = jnp.where(dx < 2, 2 - dx, 3 * (3 - dx))
+        return (z // 2 + dq) % 4, (x + dx) % NX
+
     @pl.loop(0, 16)
     def _(n):
-        q, xd = n // NX, n % NX
+        q, xd = far_first(n)
         mine = jnp.logical_and(is_root, jnp.logical_and(q == quarter, xd == x))
 
         @pl.when(mine)
@@ -165,15 +176,18 @@
             device_id=(((x + d) % NX) * 2 + core, partner(u)), device_id_type=MESH,
         )
 
-    for u in range(TC):
-        @pl.when(partner(u) % NR == r)
+    def send_ucol():
+        for u in range(TC):
+            @pl.when(partner(u) % NR == r)
+            def _():
+                for d in (2, 1, 3):
+                    ucol_to(u, d).start()
+
+        @pl.when(is_root)
         def _():
-            for d in (2, 1, 3):
-                ucol_to(u, d).start()
-
-    @pl.when(is_root)
-    def _():
-        pltpu.make_async_copy(u_hbm.at[:, quarter], u_col, ucol_recv).start()
+            pltpu.make_async_copy(u_hbm.at[:, quarter], u_col, ucol_recv).start()
+
+    send_ucol()
 
     def fz_to(rnd, way):
         sign = 1 if way == 0 else NZ - 1
@@ -458,10 +472,6 @@
                 if dx or dk or dy:
                     near.append((min(dx, NX - dx) + min(dy, NY - dy) + 0.1 * dk, dx, dk, dy))
     near.sort(reverse=True)
-    xs = [((x + d) % NX) * 2 for d in range(NX)]
-    ks = [core, 1 - core]
-    ys = [(y + d) % NY for d in range(NY)]
-
     def to_near(stage, src, dst):
         out = []
         for _, dx, dk, dy in near:
@@ -561,7 +571,7 @@
     wait_all(m5, NR * NY - 1, m_send.at[2])
     @pl.loop(0, 16)
     def _(n):
-        q, xd = n // NX, n % NX
+        q, xd = far_first(n)
         mine = jnp.logical_and(is_root, jnp.logical_and(q == quarter, xd == x))
 
         @pl.when(jnp.logical_not(mine))

time: 77.7 us -> 76 us (0.978)
  Pallas kernels: 77 us -> 75.3 us
    pallas_call x1, Pallas kernels: 74.7 us -> 73.1 us  [local(): pl.pallas_call(kernel, out_shape=(jax.ShapeDtypeStruct((128, 256), F32),...]
where the time goes in v5:
time: 76 us; the launch traced here: 75.9 us
  Pallas kernels  75.3 us (99%)
    pallas_call x1, Pallas kernels, local(): pl.pallas_call(kernel, out_shape=(jax.ShapeDtypeStruct((128, 256), F32),...  73.1 us
    pallas_call x1, Pallas kernels, local(): pl.pallas_call(finish, out_shape=(jax.ShapeDtypeStruct((128, 256), F32),...  2.23 us

profile of v5, /device:TPU:1, one launch (start us, length us, event | category | flops | bytes accessed | tf_op | source)
XLA Modules:
  0.0 75.9 jit_solution(14412156186845494974)
XLA Ops:
  0.6 73.1 %panel_step.1 = (f32[128,256]{1,0:T(8,128)}, f32[32,8,256]{2,1,0:T(8,128)}, f32[1,2]{1,0:T(1,128)}) custom-call(bf16[4,4,256,256]{3,2,1,0:T(8,128)(2,1)} %bitcast.13, bf16[32768,128]{1,0:T(8,128)(2,1)} %bitcast.12, bf16[128,256]{1,0:T(8,128)(2,1)} %bitcast.15, bf16[128,256]{1,0:T(8,128)(2,1)} %bitcast.16, f32[256,256]{1,0:T(8,128)} %b_ref.1, ...), custom_call_target="tpu_custom_call" | custom-call | flops 4294967296 | bytes 12582912 | tf_op jit(solution)/shard_map/panel_step/pallas_call | solution.py:623
  73.7 2.2 %finish.1 = (f32[128,256]{1,0:T(8,128)}, f32[256,256]{1,0:T(8,128)}, f32[1,2]{1,0:T(1,128)}) custom-call(f32[128,256]{1,0:T(8,128)} %get-tuple-element.9.adj_in, f32[256,256]{1,0:T(8,128)} %bitcast.11, f32[1,2]{1,0:T(1,128)} %get-tuple-element.11.slope_in, f32[256,256]{1,0:T(8,128)} %b_ref.1), custom_call_target="tpu_custom_call" | custom-call | tf_op jit(solution)/shard_map/finish/pallas_call | solution.py:700

commit v6 on v5

--- a/solution.py
+++ b/solution.py
@@ -146,28 +146,26 @@
 
     pl.semaphore_wait(barrier, 16 + 31 + 7 - jnp.where(is_root, 1, 0) + jnp.where(feeds, 3, 0))
 
-    def far_first(n):
-        dq, dx = n // NX, n % NX
-        dq = jnp.where(dq < 2, 2 - dq, 3 * (3 - dq))
-        dx = jnp.where(dx < 2, 2 - dx, 3 * (3 - dx))
-        return (z // 2 + dq) % 4, (x + dx) % NX
-
-    @pl.loop(0, 16)
-    def _(n):
-        q, xd = far_first(n)
-        mine = jnp.logical_and(is_root, jnp.logical_and(q == quarter, xd == x))
-
-        @pl.when(mine)
-        def _():
-            pltpu.make_async_copy(f_parts.at[q], f_buf.at[c % 2, c // 2], f_recv.at[0]).start()
-
-        @pl.when(jnp.logical_not(mine))
-        def _():
-            pltpu.make_async_remote_copy(
-                src_ref=f_parts.at[q], dst_ref=f_buf.at[c % 2, c // 2],
-                send_sem=f_send.at[n], recv_sem=f_recv.at[0],
-                device_id=(2 * xd + c % 2, NR * q + r), device_id_type=MESH,
-            ).start()
+    def rows_to(dq, dx):
+        q = (z // 2 + dq) % 4
+        return pltpu.make_async_remote_copy(
+            src_ref=f_parts.at[q], dst_ref=f_buf.at[c % 2, c // 2],
+            send_sem=f_send.at[NX * dq + dx], recv_sem=f_recv.at[0],
+            device_id=(xs[dx] + c % 2, NR * q + r), device_id_type=MESH,
+        )
+
+    for dq in (2, 1, 3, 0):
+        for dx in (2, 1, 3, 0):
+            if dq or dx:
+                rows_to(dq, dx).start()
+
+    @pl.when(is_root)
+    def _():
+        pltpu.make_async_copy(f_parts.at[quarter], f_buf.at[c % 2, c // 2], f_recv.at[0]).start()
+
+    @pl.when(jnp.logical_not(is_root))
+    def _():
+        rows_to(0, 0).start()
 
     def ucol_to(u, d):
         return pltpu.make_async_remote_copy(
@@ -562,25 +560,17 @@
     adj_copy.start()
 
     sum_third()
-    wait_all(m5, NR * NY - 1, m_recv.at[2])
-    moment_ref[...] = m5[...]
-
     adj_copy.wait()
     wait_all(m1r, NR * NY - 1, m_send.at[0])
     wait_all(m3, NZ - 1, m_send.at[1])
-    wait_all(m5, NR * NY - 1, m_send.at[2])
-    @pl.loop(0, 16)
-    def _(n):
-        q, xd = far_first(n)
-        mine = jnp.logical_and(is_root, jnp.logical_and(q == quarter, xd == x))
-
-        @pl.when(jnp.logical_not(mine))
-        def _():
-            pltpu.make_async_remote_copy(
-                src_ref=f_parts.at[q], dst_ref=f_buf.at[c % 2, c // 2],
-                send_sem=f_send.at[n], recv_sem=f_recv.at[0],
-                device_id=(2 * xd + c % 2, NR * q + r), device_id_type=MESH,
-            ).wait_send()
+    for dq in range(4):
+        for dx in range(NX):
+            if dq or dx:
+                rows_to(dq, dx).wait_send()
+
+    @pl.when(jnp.logical_not(is_root))
+    def _():
+        rows_to(0, 0).wait_send()
 
     @pl.when(feeds)
     def _():
@@ -601,6 +591,9 @@
                 for way in range(2):
                     copy_of(g, axis, rnd, way).wait_send()
 
+    wait_all(m5, NR * NY - 1, m_recv.at[2])
+    moment_ref[...] = m5[...]
+    wait_all(m5, NR * NY - 1, m_send.at[2])
 
 def finish(adj_in, m_in, slope_in, b_ref, adj_ref, diag_ref, slope_ref):
     adj_ref[...] = adj_in[...]

time: 76 us -> 75.4 us (level)
  no operation moved by 1% of the time
where the time goes in v6:
time: 75.4 us; the launch traced here: 75.2 us
  Pallas kernels  74.6 us (99%)
    pallas_call x1, Pallas kernels, local(): pl.pallas_call(kernel, out_shape=(jax.ShapeDtypeStruct((128, 256), F32),...  72.4 us
    pallas_call x1, Pallas kernels, local(): pl.pallas_call(finish, out_shape=(jax.ShapeDtypeStruct((128, 256), F32),...  2.23 us

profile of v6, /device:TPU:1, one launch (start us, length us, event | category | flops | bytes accessed | tf_op | source)
XLA Modules:
  0.0 75.2 jit_solution(5477969086099822730)
XLA Ops:
  0.6 72.4 %panel_step.1 = (f32[128,256]{1,0:T(8,128)}, f32[32,8,256]{2,1,0:T(8,128)}, f32[1,2]{1,0:T(1,128)}) custom-call(bf16[4,4,256,256]{3,2,1,0:T(8,128)(2,1)} %bitcast.13, bf16[32768,128]{1,0:T(8,128)(2,1)} %bitcast.12, bf16[128,256]{1,0:T(8,128)(2,1)} %bitcast.15, bf16[128,256]{1,0:T(8,128)(2,1)} %bitcast.16, f32[256,256]{1,0:T(8,128)} %b_ref.1, ...), custom_call_target="tpu_custom_call" | custom-call | flops 4294967296 | bytes 12582912 | tf_op jit(solution)/shard_map/panel_step/pallas_call | solution.py:616
  73.0 2.2 %finish.1 = (f32[128,256]{1,0:T(8,128)}, f32[256,256]{1,0:T(8,128)}, f32[1,2]{1,0:T(1,128)}) custom-call(f32[128,256]{1,0:T(8,128)} %get-tuple-element.9.adj_in, f32[256,256]{1,0:T(8,128)} %bitcast.11, f32[1,2]{1,0:T(1,128)} %get-tuple-element.11.slope_in, f32[256,256]{1,0:T(8,128)} %b_ref.1), custom_call_target="tpu_custom_call" | custom-call | tf_op jit(solution)/shard_map/finish/pallas_call | solution.py:693

commit v7 on v6

--- a/solution.py
+++ b/solution.py
@@ -550,6 +550,8 @@
         elif event[0] == "sum2":
             sum_second()
 
+    sum_third()
+
     for t in range(TR):
         total[pl.ds(t * 8, 8), :] = (
             c_ref[pl.ds((t // 2) * 16, 16), :].astype(F32)[(t % 2) * 8 : (t % 2) * 8 + 8]
@@ -559,7 +561,6 @@
     adj_copy = pltpu.make_async_copy(adj_ref, adj_hbm, in_sem.at[4])
     adj_copy.start()
 
-    sum_third()
     adj_copy.wait()
     wait_all(m1r, NR * NY - 1, m_send.at[0])
     wait_all(m3, NZ - 1, m_send.at[1])

time: 75.4 us -> 75 us (level)
  no operation moved by 1% of the time
where the time goes in v7:
time: 75 us; the launch traced here: 74.9 us
  Pallas kernels  74.2 us (99%)
    pallas_call x1, Pallas kernels, local(): pl.pallas_call(kernel, out_shape=(jax.ShapeDtypeStruct((128, 256), F32),...  72 us
    pallas_call x1, Pallas kernels, local(): pl.pallas_call(finish, out_shape=(jax.ShapeDtypeStruct((128, 256), F32),...  2.23 us

profile of v7, /device:TPU:1, one launch (start us, length us, event | category | flops | bytes accessed | tf_op | source)
XLA Modules:
  0.0 74.9 jit_solution(5038546995563776728)
XLA Ops:
  0.6 72.0 %panel_step.1 = (f32[128,256]{1,0:T(8,128)}, f32[32,8,256]{2,1,0:T(8,128)}, f32[1,2]{1,0:T(1,128)}) custom-call(bf16[4,4,256,256]{3,2,1,0:T(8,128)(2,1)} %bitcast.13, bf16[32768,128]{1,0:T(8,128)(2,1)} %bitcast.12, bf16[128,256]{1,0:T(8,128)(2,1)} %bitcast.15, bf16[128,256]{1,0:T(8,128)(2,1)} %bitcast.16, f32[256,256]{1,0:T(8,128)} %b_ref.1, ...), custom_call_target="tpu_custom_call" | custom-call | flops 4294967296 | bytes 12582912 | tf_op jit(solution)/shard_map/panel_step/pallas_call | solution.py:617
  72.6 2.2 %finish.1 = (f32[128,256]{1,0:T(8,128)}, f32[256,256]{1,0:T(8,128)}, f32[1,2]{1,0:T(1,128)}) custom-call(f32[128,256]{1,0:T(8,128)} %get-tuple-element.9.adj_in, f32[256,256]{1,0:T(8,128)} %bitcast.11, f32[1,2]{1,0:T(1,128)} %get-tuple-element.11.slope_in, f32[256,256]{1,0:T(8,128)} %b_ref.1), custom_call_target="tpu_custom_call" | custom-call | tf_op jit(solution)/shard_map/finish/pallas_call | solution.py:694
